TPU v7x, 32 devices: a whole 2x2x4 slice. The times are simulated.
32 devices in a mesh: blk: 8 (over y, x, core), head: 4 (over z).
Axes of the slice: x: 2, y: 2, z: 4, core: 2. Of those that a mesh axis runs over, the one named last changes fastest.
Arguments:
- tokens: bfloat16 [4096, 768], P(('blk', 'head')), may hold values from -6 to 6
- w_qkv: bfloat16 [768, 2304], P('blk', 'head'), may hold values from -0.21875 to 0.21875
- w_out: bfloat16 [768, 768], P('head', 'blk'), may hold values from -0.875 to 0.875
- w_gate_up: bfloat16 [2, 768, 3072], P(None, 'blk', 'head'), may hold values from -0.21875 to 0.21875
- w_down: bfloat16 [3072, 768], P('head', 'blk'), may hold values from -0.109375 to 0.109375
- norm_params: bfloat16 [768, 4], P('blk', 'head'), may hold values from 0.25 to 1.75
- alibi_slope: float32 [12], replicated, may hold values from 0.00012207031 to 0.001953125
- lengths: int32 [8], replicated, may hold values from 1 to 2048, 4096 in all
- placement: int32 [4096], replicated, may hold values from 0 to 4095, as said below
- out_grad: bfloat16 [4096, 768], P(('blk', 'head')), may hold values from -6 to 6
Outputs:
- activations: bfloat16 [4096, 768], P(('blk', 'head'))
- input_grad: float32 [4096, 768], P(('blk', 'head'))
- grad_qkv: float32 [768, 2304], P('blk', 'head')
- grad_out: float32 [768, 768], P('head', 'blk')
- grad_gate_up: float32 [2, 768, 3072], P(None, 'blk', 'head')
- grad_down: float32 [3072, 768], P('head', 'blk')
- grad_norm: float32 [768, 4], P('blk', 'head')
Inputs may be any that keep to these rules, and one draw needn't show every extreme that they name: `placement`: A permutation of the positions: the row at slot s of a device's 128 rows holds a position from s * 32 to (s + 1) * 32 - 1, and each such run of positions has exactly one on every device.
All inputs are finite; a program needn't handle non-finite values.
Results may differ from a plain program's by a relative error of at most 0.023.
Values may be sent and summed in bfloat16 or wider, within the bound.
A program may use at most 128 MiB of HBM per device.

v0:
```python
import jax
import jax.numpy as jnp
from jax import lax
from jax.experimental import pallas as pl
from jax.experimental.pallas import tpu as pltpu
from jax.sharding import PartitionSpec as P

HEADS = 12
HEAD_DIM = 64


masked_score = -1e30


def layer_norm(residual, norm_gain, norm_shift):
    center = residual - jnp.mean(residual, axis=-1, keepdims=True)
    spread = jnp.mean(center * center, axis=-1, keepdims=True)
    return center * lax.rsqrt(spread + 1e-05) * norm_gain + norm_shift


def geglu(gate, upward):
    return jax.nn.gelu(gate, approximate=False) * upward


def dot_back(grad_rows, weight):
    return lax.dot_general(
        grad_rows, weight, (((1,), (1,)), ((), ())), preferred_element_type=jnp.float32
    )


def weight_grad(left, right):
    return lax.dot_general(
        left, right, (((0,), (0,)), ((), ())), preferred_element_type=jnp.float32
    )


def seq_of(positions, seq_ends):
    return jnp.sum((positions[:, None] >= seq_ends[None, :]).astype(jnp.int32), axis=1)


def prefix_sums(lengths):
    count = lengths.shape[0]
    upto = jnp.arange(count)[None, :] <= jnp.arange(count)[:, None]
    return jnp.sum(jnp.where(upto, lengths[None, :], 0), axis=1)


def biased_scores(queries, key_rows, q_pos, k_pos, q_seq, k_seq, slopes, qk_scale):
    scores = (
        jnp.einsum("qhd,khd->hqk", queries, key_rows, preferred_element_type=jnp.float32) * qk_scale
    )
    distance = jnp.abs(q_pos[:, None] - k_pos[None, :]).astype(jnp.float32)
    scores = scores - slopes[:, None, None] * distance[None]
    same_seq = (q_seq[:, None] == k_seq[None, :])[None]
    return (scores, same_seq)


def shards(
    tokens, w_qkv, w_out, w_gate_up, w_down, norm_params, alibi_slope, lengths, placement, out_grad
):
    heads_n = lax.axis_size("head")
    head_idx = lax.axis_index("head")
    blk_idx = lax.axis_index("blk")
    tok_rows = tokens.shape[0]
    per_dev = HEADS // heads_n
    group_rows = heads_n * tok_rows
    qk_scale = HEAD_DIM ** (-0.5)
    group_tokens, norm_cols = (
        lax.all_gather(tokens, "head", axis=0, tiled=True),
        lax.all_gather(norm_params, "head", axis=1, tiled=True),
    )
    f_qkv, f_out, f_gu, f_down, f_norm = (
        lax.all_gather(w_qkv, "blk", axis=0, tiled=True),
        lax.all_gather(w_out, "blk", axis=1, tiled=True),
        lax.all_gather(w_gate_up, "blk", axis=1, tiled=True),
        lax.all_gather(w_down, "blk", axis=1, tiled=True),
        lax.all_gather(norm_cols, "blk", axis=0, tiled=True),
    )
    grouped = jnp.dot(group_tokens, f_qkv, preferred_element_type=jnp.float32).astype(jnp.bfloat16)
    grouped = grouped.reshape(group_rows, per_dev, 3, HEAD_DIM)
    norms = f_norm.astype(jnp.float32)
    queries = grouped[:, :, 0]
    key_rows = grouped[:, :, 1]
    values = grouped[:, :, 2]
    seq_ends = prefix_sums(lengths)
    q_pos = lax.dynamic_slice_in_dim(placement, blk_idx * group_rows, group_rows)
    q_seq = seq_of(q_pos, seq_ends)
    slopes = lax.dynamic_slice_in_dim(alibi_slope, head_idx * per_dev, per_dev)

    def split_rows(shard_part):
        block_count = shard_part[0].shape[0] // group_rows
        pieces = tuple(
            (arr.reshape((block_count, group_rows) + arr.shape[1:]) for arr in shard_part)
        )
        starts = group_rows * jnp.arange(block_count, dtype=jnp.int32)
        return pieces + (starts,)

    start_state = (
        jnp.full((per_dev, group_rows), masked_score, jnp.float32),
        jnp.zeros((per_dev, group_rows), jnp.float32),
        jnp.zeros((group_rows, per_dev, HEAD_DIM), jnp.float32),
    )
    running = start_state

    def forward_per_block(state, block_in):
        k_blk, v_blk, k_first = block_in
        row_best, row_total, out_sum = state
        k_pos = lax.dynamic_slice_in_dim(placement, k_first, group_rows)
        scores, same_seq = biased_scores(
            queries, k_blk, q_pos, k_pos, q_seq, seq_of(k_pos, seq_ends), slopes, qk_scale
        )
        row_top = jnp.max(jnp.where(same_seq, scores, masked_score), axis=2)
        new_best = jnp.maximum(row_best, row_top)
        factor = jnp.exp(row_best - new_best)
        prob_tile = jnp.where(same_seq, jnp.exp(scores - new_best[:, :, None]), 0.0)
        row_total = row_total * factor + jnp.sum(prob_tile, axis=2)
        out_sum = out_sum * factor.T[:, :, None] + jnp.einsum(
            "hqk,khd->qhd",
            prob_tile.astype(jnp.bfloat16),
            v_blk,
            preferred_element_type=jnp.float32,
        )
        return ((new_best, row_total, out_sum), None)

    running, _ = lax.scan(
        forward_per_block,
        running,
        split_rows(
            (
                lax.all_gather(key_rows, "blk", axis=0, tiled=True),
                lax.all_gather(values, "blk", axis=0, tiled=True),
            )
        ),
    )
    row_best, row_total, out_sum = running
    attended = (out_sum / row_total.T[:, :, None]).astype(jnp.bfloat16)
    log_total = row_best + jnp.log(row_total)
    mixed = attended.reshape(group_rows, per_dev * HEAD_DIM)
    attn_out = lax.psum_scatter(
        jnp.dot(mixed, f_out, preferred_element_type=jnp.float32).astype(jnp.bfloat16),
        "head",
        scatter_dimension=0,
        tiled=True,
    ).astype(jnp.float32)
    resid_one = tokens.astype(jnp.float32) + attn_out
    hidden, norm_one_back = jax.vjp(layer_norm, resid_one, norms[:, 0], norms[:, 1])
    hidden_low = hidden.astype(jnp.bfloat16)
    ffn_rows = lax.all_gather(hidden_low, "head", axis=0, tiled=True)
    gate = jnp.dot(ffn_rows, f_gu[0], preferred_element_type=jnp.float32)
    upward = jnp.dot(ffn_rows, f_gu[1], preferred_element_type=jnp.float32)
    gated, geglu_back = jax.vjp(geglu, gate, upward)
    gated_low = gated.astype(jnp.bfloat16)
    branch_part = jnp.dot(gated_low, f_down, preferred_element_type=jnp.float32)
    branch = lax.psum_scatter(
        branch_part.astype(jnp.bfloat16), "head", scatter_dimension=0, tiled=True
    ).astype(jnp.float32)
    result, norm_two_back = jax.vjp(layer_norm, hidden + branch, norms[:, 2], norms[:, 3])
    d_two, d_gain_two, d_shift_two = norm_two_back(out_grad.astype(jnp.float32))
    d_branch = d_two.astype(jnp.bfloat16)
    branch_rows = lax.all_gather(d_branch, "head", axis=0, tiled=True)
    g_down = weight_grad(gated_low, branch_rows)
    d_gate, d_up = geglu_back(dot_back(branch_rows, f_down))
    d_gate_low = d_gate.astype(jnp.bfloat16)
    d_up_low = d_up.astype(jnp.bfloat16)
    g_gate_up = jnp.stack([weight_grad(ffn_rows, d_gate_low), weight_grad(ffn_rows, d_up_low)])
    hidden_part = dot_back(d_gate_low, f_gu[0]) + dot_back(d_up_low, f_gu[1])
    d_hidden = d_two + lax.psum_scatter(
        hidden_part.astype(jnp.bfloat16), "head", scatter_dimension=0, tiled=True
    ).astype(jnp.float32)
    d_one, d_gain_one, d_shift_one = norm_one_back(d_hidden)
    d_attn = d_one.astype(jnp.bfloat16)
    attn_rows = lax.all_gather(d_attn, "head", axis=0, tiled=True)
    g_out = weight_grad(mixed, attn_rows)
    d_heads = dot_back(attn_rows, f_out).astype(jnp.bfloat16).reshape(group_rows, per_dev, HEAD_DIM)
    delta = jnp.sum(d_heads.astype(jnp.float32) * attended.astype(jnp.float32), axis=2).T
    zero_grad = jnp.zeros((group_rows, per_dev, HEAD_DIM), jnp.float32)
    grad_q = zero_grad

    def query_per_block(running, block_in):
        k_blk, v_blk, k_first = block_in
        k_pos = lax.dynamic_slice_in_dim(placement, k_first, group_rows)
        scores, same_seq = biased_scores(
            queries, k_blk, q_pos, k_pos, q_seq, seq_of(k_pos, seq_ends), slopes, qk_scale
        )
        prob_tile = jnp.where(same_seq, jnp.exp(scores - log_total[:, :, None]), 0.0)
        d_prob = jnp.einsum("qhd,khd->hqk", d_heads, v_blk, preferred_element_type=jnp.float32)
        d_score = (prob_tile * (d_prob - delta[:, :, None])).astype(jnp.bfloat16)
        running = (
            running
            + jnp.einsum("hqk,khd->qhd", d_score, k_blk, preferred_element_type=jnp.float32)
            * qk_scale
        )
        return (running, None)

    grad_q, _ = lax.scan(
        query_per_block,
        grad_q,
        split_rows(
            (
                lax.all_gather(key_rows, "blk", axis=0, tiled=True),
                lax.all_gather(values, "blk", axis=0, tiled=True),
            )
        ),
    )
    stats_lse, stats_delta = (
        lax.all_gather(log_total, "blk", axis=1, tiled=True),
        lax.all_gather(delta, "blk", axis=1, tiled=True),
    )
    running = (zero_grad, zero_grad)

    def key_per_block(state, block_in):
        q_blk, do_blk, q_first = block_in
        grad_k, grad_v = state
        other_pos = lax.dynamic_slice_in_dim(placement, q_first, group_rows)
        lse_blk = lax.dynamic_slice_in_dim(stats_lse, q_first, group_rows, 1)
        delta_blk = lax.dynamic_slice_in_dim(stats_delta, q_first, group_rows, 1)
        scores, same_seq = biased_scores(
            q_blk, key_rows, other_pos, q_pos, seq_of(other_pos, seq_ends), q_seq, slopes, qk_scale
        )
        prob_tile = jnp.where(same_seq, jnp.exp(scores - lse_blk[:, :, None]), 0.0)
        grad_v = grad_v + jnp.einsum(
            "hqk,qhd->khd",
            prob_tile.astype(jnp.bfloat16),
            do_blk,
            preferred_element_type=jnp.float32,
        )
        d_prob = jnp.einsum("qhd,khd->hqk", do_blk, values, preferred_element_type=jnp.float32)
        d_score = (prob_tile * (d_prob - delta_blk[:, :, None])).astype(jnp.bfloat16)
        grad_k = (
            grad_k
            + jnp.einsum("hqk,qhd->khd", d_score, q_blk, preferred_element_type=jnp.float32)
            * qk_scale
        )
        return ((grad_k, grad_v), None)

    running, _ = lax.scan(
        key_per_block,
        running,
        split_rows(
            (
                lax.all_gather(queries, "blk", axis=0, tiled=True),
                lax.all_gather(d_heads, "blk", axis=0, tiled=True),
            )
        ),
    )
    grad_k, grad_v = running
    d_grouped = jnp.stack([grad_q, grad_k, grad_v], axis=2).astype(jnp.bfloat16)
    g_norm = jnp.stack([d_gain_one, d_shift_one, d_gain_two, d_shift_two], axis=1)
    d_qkv = d_grouped.reshape(group_rows, per_dev * 3 * HEAD_DIM)
    g_qkv = weight_grad(group_tokens, d_qkv)
    input_sum, norm_share = (
        lax.psum_scatter(
            dot_back(d_qkv, f_qkv).astype(jnp.bfloat16), "head", scatter_dimension=0, tiled=True
        ).astype(jnp.float32),
        lax.psum_scatter(
            g_norm.astype(jnp.bfloat16), "head", scatter_dimension=1, tiled=True
        ).astype(jnp.float32),
    )
    input_grad = d_one + input_sum
    s_qkv, s_out, s_gu, s_down, s_norm = (
        lax.psum_scatter(g_qkv, "blk", scatter_dimension=0, tiled=True),
        lax.psum_scatter(g_out, "blk", scatter_dimension=1, tiled=True),
        lax.psum_scatter(g_gate_up, "blk", scatter_dimension=1, tiled=True),
        lax.psum_scatter(g_down, "blk", scatter_dimension=1, tiled=True),
        lax.psum_scatter(norm_share, "blk", scatter_dimension=0, tiled=True),
    )
    return (result.astype(jnp.bfloat16), input_grad, s_qkv, s_out, s_gu, s_down, s_norm)


Q_SLOTS = 32
K_SLOTS = 16
SEQ_STEP = 65536.0
FAR = 32768.0
LANE_OF = (0, 64, 192)


def by_head(rows, lanes):
    lane = lax.broadcasted_iota(jnp.int32, rows.shape, 1)
    parts = [jnp.where((lane >= first) & (lane < first + HEAD_DIM), rows, 0.0) for first in lanes]
    return jnp.concatenate(parts, axis=0).astype(jnp.bfloat16)


def key_tiles(kv_ref, j):
    rows = kv_ref.shape[0] * K_SLOTS
    blk = kv_ref[:, pl.ds(pl.multiple_of(j * K_SLOTS, K_SLOTS), K_SLOTS), :]
    return blk.reshape(rows, blk.shape[2])


def key_span(len_ref, i, devs):
    first = i * (Q_SLOTS * devs)
    last = first + Q_SLOTS * devs - 1
    end, low, high = 0, 0, 0
    for k in range(8):
        start = end
        end = end + len_ref[k]
        low = jnp.where((first >= start) & (first < end), start, low)
        high = jnp.where((last >= start) & (last < end), end, high)
    step = K_SLOTS * devs
    return low // step, (high + step - 1) // step


def attend(len_ref, slope_ref, q_ref, kv_ref, kcode_ref, qcode_ref, out_ref, lse_ref, vt_ref):
    z = lax.axis_index("head")
    devs, slots, _ = kv_ref.shape
    rows = devs * K_SLOTS
    q_rows = q_ref.shape[0] * Q_SLOTS

    def turn(j, _):
        kv = key_tiles(kv_ref, j)[:, 128:384]
        vt_ref[j] = kv.T
        return 0

    lax.fori_loop(0, slots // K_SLOTS, turn, 0)

    def chunk(i, _):
        first = pl.multiple_of(i * Q_SLOTS, Q_SLOTS)
        q = q_ref[:, pl.ds(first, Q_SLOTS), :].reshape(q_rows, 256).astype(jnp.float32)
        qbd = by_head(q, (0, 64, 128))
        qcode = qcode_ref[i, 0:1, :]
        lo, hi = key_span(len_ref, i, devs)

        def block(j, state):
            kv = key_tiles(kv_ref, j)
            keys = jnp.concatenate([kv[:, 0:128], kv[:, 256:384]], axis=1)
            s_all = lax.dot_general(keys, qbd, (((1,), (1,)), ((), ())), preferred_element_type=jnp.float32)
            dist = jnp.abs(key_tiles(kcode_ref, j) - qcode)
            keep = dist < FAR
            fresh = []
            for h in range(3):
                best, total, acc = state[h]
                s = jnp.where(keep, s_all[:, 128 * h : 128 * h + 128] - slope_ref[3 * z + h] * dist, masked_score)
                top = jnp.maximum(best, jnp.max(s, axis=0, keepdims=True))
                factor = jnp.exp(best - top)
                p = jnp.exp(s - top)
                total = total * factor + jnp.sum(p, axis=0, keepdims=True)
                vt = vt_ref[j, LANE_OF[h] : LANE_OF[h] + 64, :]
                acc = acc * factor + jnp.dot(vt, p.astype(jnp.bfloat16), preferred_element_type=jnp.float32)
                fresh.append((top, total, acc))
            return tuple(fresh)

        start = tuple(
            (
                jnp.full((1, q_rows), masked_score, jnp.float32),
                jnp.zeros((1, q_rows), jnp.float32),
                jnp.zeros((64, q_rows), jnp.float32),
            )
            for _ in range(3)
        )
        done = lax.fori_loop(lo, hi, block, start)
        outs = [acc / total for _, total, acc in done]
        full = jnp.concatenate([outs[0], outs[1], jnp.zeros((64, q_rows), jnp.float32), outs[2]], axis=0)
        out_ref[:, pl.ds(first, Q_SLOTS), :] = full.T.astype(jnp.bfloat16).reshape(-1, Q_SLOTS, 256)
        for h in range(3):
            lse_ref[i, h : h + 1, :] = done[h][0] + jnp.log(done[h][1])
        return 0

    lax.fori_loop(0, slots // Q_SLOTS, chunk, 0)


def attend_back(len_ref, slope_ref, q_ref, kv_ref, kcode_ref, qcode_ref, out_ref, do_ref, lse_ref, act_any, sdown_any,
                dq_ref, dkv_ref, act_out, sdown_out, kt_ref, sum_ref, sem):
    z = lax.axis_index("head")
    devs, slots, _ = kv_ref.shape
    rows = devs * K_SLOTS
    q_rows = q_ref.shape[0] * Q_SLOTS
    scale = HEAD_DIM ** (-0.5)
    along = [
        pltpu.make_async_copy(act_any, act_out, sem.at[0]),
        pltpu.make_async_copy(sdown_any, sdown_out, sem.at[1]),
    ]
    for c in along:
        c.start()

    def turn(j, _):
        kv = key_tiles(kv_ref, j)
        keys = jnp.concatenate([kv[:, 0:128], kv[:, 256:384]], axis=1)
        kt_ref[j] = keys.T
        sum_ref[j] = jnp.zeros((rows, 384), jnp.float32)
        return 0

    lax.fori_loop(0, slots // K_SLOTS, turn, 0)

    def chunk(i, _):
        first = pl.multiple_of(i * Q_SLOTS, Q_SLOTS)
        q = q_ref[:, pl.ds(first, Q_SLOTS), :].reshape(q_rows, 256).astype(jnp.float32)
        qbd = by_head(q, (0, 64, 128))
        do = do_ref[:, pl.ds(first, Q_SLOTS), :].reshape(q_rows, 256).astype(jnp.float32)
        out = out_ref[:, pl.ds(first, Q_SLOTS), :].reshape(q_rows, 256).astype(jnp.float32)
        dobd = by_head(do, LANE_OF)
        prod = (do * out).T
        delta = [jnp.sum(prod[f : f + 64, :], axis=0, keepdims=True) for f in LANE_OF]
        qcode = qcode_ref[i, 0:1, :]
        lo, hi = key_span(len_ref, i, devs)

        def block(j, state):
            kv = key_tiles(kv_ref, j)
            keys = jnp.concatenate([kv[:, 0:128], kv[:, 256:384]], axis=1)
            vals = kv[:, 128:384]
            s_all = lax.dot_general(keys, qbd, (((1,), (1,)), ((), ())), preferred_element_type=jnp.float32)
            dp_all = lax.dot_general(vals, dobd, (((1,), (1,)), ((), ())), preferred_element_type=jnp.float32)
            dist = jnp.abs(key_tiles(kcode_ref, j) - qcode)
            keep = dist < FAR
            ps, dss, fresh = [], [], []
            for h in range(3):
                s = s_all[:, 128 * h : 128 * h + 128] - slope_ref[3 * z + h] * dist - lse_ref[i, h : h + 1, :]
                p = jnp.exp(jnp.where(keep, s, masked_score))
                ds = (p * (dp_all[:, 128 * h : 128 * h + 128] - delta[h])).astype(jnp.bfloat16)
                ps.append(p.astype(jnp.bfloat16))
                dss.append(ds)
                kt = kt_ref[j, 64 * h : 64 * h + 64, :]
                fresh.append(state[h] + jnp.dot(kt, ds, preferred_element_type=jnp.float32))
            dv = jnp.dot(jnp.concatenate(ps, axis=1), dobd, preferred_element_type=jnp.float32)
            dk = jnp.dot(jnp.concatenate(dss, axis=1), qbd, preferred_element_type=jnp.float32)
            sum_ref[j, :, 0:128] += dk[:, 0:128]
            sum_ref[j, :, 128:256] += dv[:, 0:128]
            sum_ref[j, :, 256:384] += dk[:, 128:256] + dv[:, 128:256]
            return tuple(fresh)

        start = tuple(jnp.zeros((64, q_rows), jnp.float32) for _ in range(3))
        done = lax.fori_loop(lo, hi, block, start)
        full = jnp.concatenate(done + (jnp.zeros((64, q_rows), jnp.float32),), axis=0) * scale
        dq_ref[:, pl.ds(first, Q_SLOTS), :] = full.T.astype(jnp.bfloat16).reshape(-1, Q_SLOTS, 256)
        return 0

    lax.fori_loop(0, slots // Q_SLOTS, chunk, 0)

    def leave(j, _):
        dkv_ref[:, pl.ds(pl.multiple_of(j * K_SLOTS, K_SLOTS), K_SLOTS), :] = (
            sum_ref[j].astype(jnp.bfloat16).reshape(devs, K_SLOTS, 384)
        )
        return 0

    lax.fori_loop(0, slots // K_SLOTS, leave, 0)
    for c in along:
        c.wait()


VM = pl.BlockSpec(memory_space=pltpu.VMEM)
SM = pl.BlockSpec(memory_space=pltpu.SMEM)
ANY = pl.BlockSpec(memory_space=pl.ANY)
HBM = pl.BlockSpec(memory_space=pltpu.MemorySpace.HBM)


def run_attend(lengths, slopes, q, kv, kcode, qcode):
    heads_n, slots, _ = q.shape
    devs = kv.shape[0]
    return pl.pallas_call(
        attend,
        out_shape=(
            jax.ShapeDtypeStruct((heads_n, slots, 256), jnp.bfloat16),
            jax.ShapeDtypeStruct((slots // Q_SLOTS, 8, heads_n * Q_SLOTS), jnp.float32),
        ),
        in_specs=[SM, SM, VM, VM, VM, VM],
        out_specs=(VM, VM),
        scratch_shapes=[pltpu.VMEM((slots // K_SLOTS, 256, devs * K_SLOTS), jnp.bfloat16)],
        compiler_params=pltpu.CompilerParams(vmem_limit_bytes=16 << 20),
        name="attend",
    )(lengths, slopes, q, kv, kcode, qcode)


def run_attend_back(lengths, slopes, q, kv, kcode, qcode, out, do, lse, act, s_down):
    heads_n, slots, _ = q.shape
    devs = kv.shape[0]
    return pl.pallas_call(
        attend_back,
        out_shape=(
            jax.ShapeDtypeStruct((heads_n, slots, 256), jnp.bfloat16),
            jax.ShapeDtypeStruct((devs, slots, 384), jnp.bfloat16),
            jax.ShapeDtypeStruct(act.shape, act.dtype),
            jax.ShapeDtypeStruct(s_down.shape, s_down.dtype),
        ),
        in_specs=[SM, SM, VM, VM, VM, VM, VM, VM, VM, ANY, ANY],
        out_specs=(VM, VM, ANY, ANY),
        scratch_shapes=[
            pltpu.VMEM((slots // K_SLOTS, 256, devs * K_SLOTS), jnp.bfloat16),
            pltpu.VMEM((slots // K_SLOTS, devs * K_SLOTS, 384), jnp.float32),
            pltpu.SemaphoreType.DMA((2,)),
        ],
        compiler_params=pltpu.CompilerParams(vmem_limit_bytes=26 << 20),
        name="attend_back",
    )(lengths, slopes, q, kv, kcode, qcode, out, do, lse, act, s_down)


MESH = pl.DeviceIdType.MESH


def dot_tn(left, right):
    return lax.dot_general(left, right, (((0,), (0,)), ((), ())), preferred_element_type=jnp.float32)


def dot_nt(left, right):
    return lax.dot_general(left, right, (((1,), (1,)), ((), ())), preferred_element_type=jnp.float32)


def greet(peers):
    barrier = pltpu.get_barrier_semaphore()
    for peer in peers:
        pl.semaphore_signal(barrier, inc=1, device_id=peer, device_id_type=MESH)
    pl.semaphore_wait(barrier, len(peers))


class Sender:
    def __init__(self, sems):
        self.sems = sems
        self.used = 0
        self.left = []

    def __call__(self, src, dst, peer, only=None, arrive=None):
        i = self.used
        self.used += 1
        assert i < self.sems.shape[1]
        copy = pltpu.make_async_remote_copy(
            src_ref=src, dst_ref=dst, send_sem=self.sems.at[0, i],
            recv_sem=self.sems.at[1, i] if arrive is None else arrive,
            device_id=peer, device_id_type=MESH,
        )
        copy.arrive = self.sems.at[1, i]
        self.left.append((copy, only))
        if only is None:
            copy.start()
        else:
            pl.when(only)(copy.start)
        return copy

    def finish(self):
        for copy, only in self.left:
            if only is None:
                copy.wait_send()
            else:
                pl.when(only)(copy.wait_send)


class Spread:
    def __init__(self, go, mid, slot, z, line):
        self.go, self.mid, self.slot, self.z, self.line = go, mid, slot, z, line
        self.two = go(slot(z), slot(z), line[2])
        self.three = go(slot(z), slot(z), line[3], only=mid)
        self.one = go(slot(z), slot(z), line[1])

    def pass_on(self):
        self.two.wait_recv()
        far = self.slot(self.z ^ 2)
        self.go(far, far, self.line[1], only=self.mid, arrive=self.three.arrive)


def finish(
    dkv_ref, dq_ref, tok_ref, w_ref, datt_ref, mixed_ref, done_ref, gn_ref, up_ref,
    dx_ref, sqkv_ref, sout_ref, snorm_ref, sup_ref,
    up_in, kv_sib, kv_sum, kv_in, g_one, g_two, g_sib, g_sum, g_in,
    part, part_in, att, dkvq, nz_in, nrow, np_in, relay, sems,
):
    b = lax.axis_index("blk")
    z = lax.axis_index("head")
    chip, core = b // 2, b % 2
    sib = (chip * 2 + 1 - core, z)
    flat = [((chip ^ r) * 2 + core, z) for r in (0, 1, 2, 3)]
    line = [(b, z ^ r) for r in (0, 1, 2, 3)]
    greet([sib] + flat[1:] + line[1:])
    f32, bf16 = jnp.float32, jnp.bfloat16
    go = Sender(sems)
    mid = (z == 1) | (z == 2)
    ends = (z == 0) | (z == 3)

    def member(r):
        return pl.ds(pl.multiple_of((z ^ r) * 128, 128), 128)

    kv_c = {
        (q, r): go(dkv_ref.at[(chip ^ r) * 2 + 1 - core, member(q)], kv_sib.at[q, r], sib)
        for q in (3, 2, 1, 0) for r in (3, 1, 2, 0)
    }
    att[z] = datt_ref[...]
    att_c = Spread(go, mid, lambda j: att.at[j], z, line)
    nz_c = [go(gn_ref.at[pl.ds((z ^ r) * 8, 8)], nz_in.at[r - 1], line[r]) for r in (1, 2, 3)]
    kv_out = {}
    for q in (3, 2, 1, 0):
        for r in (3, 1, 2, 0):
            kv_c[q, r].wait_recv()
            both = dkv_ref[(chip ^ r) * 2 + core, member(q), :].astype(f32) + kv_sib[q, r].astype(f32)
            kv_sum[q, r] = both.astype(bf16)
            if r:
                kv_out[q, r] = go(kv_sum.at[q, r], kv_in.at[q, r - 1], flat[r])
    dkvq[:, 384:640] = dq_ref[...]

    @pl.when(ends)
    def _():
        relay[...] = jnp.zeros((128, 768), bf16)
        part_in[2] = jnp.zeros((128, 768), bf16)

    up_c = [go(up_ref.at[r], up_in.at[r - 1], flat[r]) for r in (3, 1, 2)]

    def send_half(part_i, grads):
        return [
            go(grads.at[pl.ds(pl.multiple_of(((chip ^ r) * 2 + 1 - core) * 96, 96), 96)], g_sib.at[part_i, r], sib)
            for r in (3, 1, 2, 0)
        ]

    def send_sum(part_i, grads, copies):
        out = []
        for k, r in enumerate((3, 1, 2, 0)):
            copies[k].wait_recv()
            mine = grads[pl.ds(pl.multiple_of(((chip ^ r) * 2 + core) * 96, 96), 96), :].astype(f32)
            g_sum[part_i, r] = (mine + g_sib[part_i, r].astype(f32)).astype(bf16)
            if r:
                out.append(go(g_sum.at[part_i, r], g_in.at[part_i, r - 1], flat[r]))
        return out

    def settle(part_i, copies):
        for c in copies:
            c.wait_recv()
        return (
            g_sum[part_i, 0].astype(f32) + g_in[part_i, 0].astype(f32)
            + g_in[part_i, 1].astype(f32) + g_in[part_i, 2].astype(f32)
        )

    att_c.pass_on()
    for c in nz_c:
        c.wait_recv()
    nrow[0] = gn_ref[pl.ds(z * 8, 8)] + nz_in[0] + nz_in[1] + nz_in[2]
    np_c = [go(nrow.at[0], np_in.at[r], flat[r]) for r in (1, 2, 3)]
    last = dot_tn(tok_ref[...], dq_ref[...])
    g_one[:, 0:128] = last[:, 0:128].astype(bf16)
    dx_c = []
    for q in (3, 2, 1, 0):
        for r in (1, 2, 3):
            kv_out[q, r].wait_recv()
        dkvq[member(q), 0:384] = (
            kv_sum[q, 0].astype(f32) + kv_in[q, 0].astype(f32) + kv_in[q, 1].astype(f32) + kv_in[q, 2].astype(f32)
        ).astype(bf16)
        term = dot_nt(dkvq[member(q), :], w_ref[...])
        if q == 3:
            part[2] = term.astype(bf16)
            passed = go(part.at[2], relay, line[1], only=ends)
            dx_three = go(part.at[2], part_in.at[2], line[3], only=mid)
        elif q == 2:
            far = term
        elif q == 1:
            part[0] = term.astype(bf16)
            dx_c.append(go(part.at[0], part_in.at[0], line[1]))
            pl.when(mid)(passed.wait_recv)
            part[1] = (far + relay[...].astype(f32)).astype(bf16)
            dx_c.append(go(part.at[1], part_in.at[1], line[2]))
        else:
            dx_ref[...] = done_ref[...] + term
    g_two[...] = dot_tn(tok_ref[...], dkvq[:, 0:384]).astype(bf16)
    two_c = send_half(1, g_two)
    att_c.one.wait_recv()
    att_c.three.wait_recv()
    outs = dot_tn(att[...].reshape(512, 768), mixed_ref[...])
    g_one[:, 128:256] = outs[:, 0:128].astype(bf16)
    g_one[:, 256:384] = (outs[:, 128:256] + last[:, 128:256]).astype(bf16)
    one_c = send_half(0, g_one)
    two_out = send_sum(1, g_two, two_c)
    one_out = send_sum(0, g_one, one_c)
    for c in np_c:
        c.wait_recv()
    nrow[1] = nrow[0] + np_in[1] + np_in[2] + np_in[3]
    half = go(nrow.at[1], np_in.at[0], sib)
    half.wait_recv()
    full = nrow[1] + np_in[0]
    snorm_ref[...] = pltpu.roll(full, lax.rem(768 - 96 * b, 768), 1)[:, 0:128]
    for c in up_c:
        c.wait_recv()
    sup_ref[...] = up_ref[0].astype(f32) + up_in[0].astype(f32) + up_in[1].astype(f32) + up_in[2].astype(f32)
    two = settle(1, two_out)
    one = settle(0, one_out)
    piece = [two[:, 64 * i : 64 * i + 64] for i in range(6)]
    piece += [one[:, 0:64], one[:, 64:128], one[:, 256:320]]
    for k, i in enumerate((6, 0, 2, 7, 1, 3, 8, 4, 5)):
        sqkv_ref[:, 64 * k : 64 * k + 64] = piece[i]
    turned = jnp.concatenate([one[:, 128:384], jnp.zeros((32, 256), f32)], axis=0).T
    sout_ref[0:128, :] = turned[0:128, 0:96]
    sout_ref[128:192, :] = turned[192:256, 0:96]
    for c in dx_c:
        c.wait_recv()
    pl.when(mid)(dx_three.wait_recv)
    dx_ref[...] += part_in[0].astype(f32) + part_in[1].astype(f32) + part_in[2].astype(f32)
    go.finish()


def run_finish(dkv, dq, toks, w, datt, mixed, done, gn, up):
    f32, bf16 = jnp.float32, jnp.bfloat16
    V = pltpu.VMEM
    return pl.pallas_call(
        finish,
        out_shape=(
            jax.ShapeDtypeStruct((128, 768), f32),
            jax.ShapeDtypeStruct((96, 576), f32),
            jax.ShapeDtypeStruct((192, 96), f32),
            jax.ShapeDtypeStruct((8, 128), f32),
            jax.ShapeDtypeStruct((96, 768), f32),
        ),
        in_specs=[VM] * 9,
        out_specs=(VM,) * 5,
        scratch_shapes=[
            V((3, 96, 768), bf16),
            V((4, 4, 128, 384), bf16), V((4, 4, 128, 384), bf16), V((4, 3, 128, 384), bf16),
            V((768, 384), bf16), V((768, 384), bf16),
            V((2, 4, 96, 384), bf16), V((2, 4, 96, 384), bf16), V((2, 3, 96, 384), bf16),
            V((3, 128, 768), bf16), V((3, 128, 768), bf16), V((4, 128, 768), bf16), V((512, 640), bf16),
            V((3, 8, 768), f32), V((2, 8, 768), f32), V((4, 8, 768), f32), V((128, 768), bf16),
            pltpu.SemaphoreType.DMA((2, 72)),
        ],
        compiler_params=pltpu.CompilerParams(
            collective_id=5, has_side_effects=True, vmem_limit_bytes=28 << 20
        ),
        name="finish",
    )(dkv, dq, toks, w, datt, mixed, done, gn, up)


def collect(
    len_any, tok_any, wq_any, wout_any, nrm_any, pos_any,
    gt, wat, q_ref, kv, wout, norm_out, kcode, qcode,
    wa_ref, wo_ref, nr, code_ref, wq_ref, wout_ref, nrm_row, pos_ref, nrm_ref, len_ref, sems, lsem,
):
    b = lax.axis_index("blk")
    z = lax.axis_index("head")
    chip, core = b // 2, b % 2
    sib = (chip * 2 + 1 - core, z)
    near = [(chip ^ r) * 2 + core for r in (0, 1, 2, 3)]
    flat = [(n, z) for n in near]
    line = [(b, z ^ r) for r in (0, 1, 2, 3)]
    f32, bf16 = jnp.float32, jnp.bfloat16
    fetch = [
        pltpu.make_async_copy(wq_any, wq_ref, lsem.at[0]),
        pltpu.make_async_copy(wout_any, wout_ref, lsem.at[1]),
        pltpu.make_async_copy(nrm_any, nrm_row, lsem.at[2]),
        pltpu.make_async_copy(pos_any, pos_ref, lsem.at[3]),
        pltpu.make_async_copy(tok_any, gt.at[z], lsem.at[4]),
        pltpu.make_async_copy(len_any, len_ref, lsem.at[5]),
    ]
    for c in fetch:
        c.start()
    for c in fetch:
        c.wait()
    go = Sender(sems)
    mid = (z == 1) | (z == 2)
    ends = (z == 0) | (z == 3)

    wq = wq_ref[...].astype(f32)
    wo = wout_ref[...].astype(f32)
    wo = jnp.concatenate([wo[0:128], jnp.zeros((64, 96), f32), wo[128:192]], axis=0)
    wo = jnp.concatenate([wo, jnp.zeros((256, 32), f32)], axis=1).T[0:96]
    wo_ref[...] = wo.astype(bf16)
    piece = [wq[:, 64 * i : 64 * i + 64] for i in range(9)] + [wo[:, 192:256]]
    for k in range(5):
        tile = jnp.concatenate([piece[PACK[2 * k]], piece[PACK[2 * k + 1]]], axis=1)
        wa_ref[:, 128 * k : 128 * k + 128] = tile.astype(bf16)
    wat[b] = wa_ref[...]
    wout[z, b] = wo_ref[...]
    nrm_ref[...] = jnp.zeros((8, 128), f32)
    nrm_ref[0:1, 0:96] = nrm_row[...].astype(f32)
    nr[b, z] = nrm_ref[...]
    greet([sib] + flat[1:] + line[1:])
    wo_z = [go(wo_ref, wout.at[z, b], line[r]) for r in (3, 2, 1)]
    nr_z = [go(nrm_ref, nr.at[b, z], line[r]) for r in (3, 2, 1)]
    wa_p = [go(wa_ref, wat.at[b], flat[r]) for r in (3, 1, 2)]
    tok_z = Spread(go, mid, lambda j: gt.at[j], z, line)
    wa_s = [go(wa_ref, wat.at[b], sib)]
    passed = []
    pos = pos_ref[...]
    seq = jnp.zeros(pos.shape, f32)
    end = 0
    for k in range(8):
        end = end + len_ref[k]
        seq = seq + jnp.where(pos >= end, 1.0, 0.0)
    code_ref[...] = pos.astype(f32) + SEQ_STEP * seq

    def spread_code(d, _):
        kcode[d] = jnp.broadcast_to(code_ref[pl.ds(d, 1), :], (128, 128)).T
        return 0

    lax.fori_loop(0, 32, spread_code, 0)
    own_code = [code_ref[pl.ds(b * 4 + j, 1), :] for j in range(4)]
    for i in range(4):
        qcode[i, 0:1, :] = jnp.concatenate([c[:, 32 * i : 32 * i + 32] for c in own_code], axis=1)
    for c in wo_z + nr_z:
        c.wait_recv()
    for k, r in enumerate((3, 1, 2)):
        wa_p[k].wait_recv()
        wa_s.append(go(wat.at[near[r]], wat.at[near[r]], sib))
    wo_p = [go(wout.at[:, b], wout.at[:, b], flat[r]) for r in (3, 1, 2)]
    passed.append(go(wout.at[:, b], wout.at[:, b], sib))
    nr_p = [go(nr.at[b], nr.at[b], flat[r]) for r in (3, 1, 2)]
    passed.append(go(nr.at[b], nr.at[b], sib))
    for c in wa_s:
        c.wait_recv()
    kv_p = []
    for r in (0, 2, 1, 3):
        if r == 2:
            tok_z.pass_on()
        elif r:
            (tok_z.one if r == 1 else tok_z.three).wait_recv()
        j = z ^ r
        rows = jnp.dot(gt[j], wat[...].reshape(768, 640), preferred_element_type=f32)
        kv[b * 4 + j] = rows[:, 0:384].astype(bf16)
        kv_p.append([go(kv.at[b * 4 + j], kv.at[b * 4 + j], flat[s]) for s in (3, 1, 2)])
        passed.append(go(kv.at[b * 4 + j], kv.at[b * 4 + j], sib))
        q_ref[j] = rows[:, 384:640].astype(bf16) * bf16(HEAD_DIM ** (-0.5))
    for k, r in enumerate((3, 1, 2)):
        wo_p[k].wait_recv()
        nr_p[k].wait_recv()
        n = near[r]
        passed.append(go(wout.at[:, n], wout.at[:, n], sib))
        passed.append(go(nr.at[n], nr.at[n], sib))
    for step, r in enumerate((0, 2, 1, 3)):
        j = z ^ r
        for k, s in enumerate((3, 1, 2)):
            kv_p[step][k].wait_recv()
            n = near[s] * 4 + j
            passed.append(go(kv.at[n], kv.at[n], sib))
    for c in passed:
        c.wait_recv()
    total = jnp.zeros((8, 768), f32)
    for n in range(8):
        rows = jnp.concatenate([nr[n, j, 0:1, :] for j in range(4)] + [jnp.zeros((4, 128), f32)], axis=0)
        total = total + pltpu.roll(jnp.concatenate([rows, jnp.zeros((8, 640), f32)], axis=1), 96 * n, 1)
    norm_out[...] = total
    go.finish()


def run_collect(lengths, tok, wq, wo, nrm, pos):
    f32, bf16 = jnp.float32, jnp.bfloat16
    S = jax.ShapeDtypeStruct
    V = pltpu.VMEM
    return pl.pallas_call(
        collect,
        out_shape=(
            S((4, 128, 768), bf16), S((8, 96, 640), bf16), S((4, 128, 256), bf16), S((32, 128, 384), bf16),
            S((4, 8, 96, 256), bf16), S((8, 768), f32), S((32, 128, 128), f32), S((4, 8, 128), f32),
        ),
        in_specs=[HBM] * 6,
        out_specs=(VM,) * 8,
        scratch_shapes=[
            V((96, 640), bf16), V((96, 256), bf16), V((8, 4, 8, 128), f32), V((32, 128), f32),
            V((96, 576), bf16), V((192, 96), bf16), V((1, 96), bf16), V((32, 128), jnp.int32), V((8, 128), f32),
            pltpu.SMEM((8,), jnp.int32), pltpu.SemaphoreType.DMA((2, 64)), pltpu.SemaphoreType.DMA((6,)),
        ],
        compiler_params=pltpu.CompilerParams(
            collective_id=1, has_side_effects=True, vmem_limit_bytes=20 << 20
        ),
        name="collect",
    )(lengths, tok, wq, wo, nrm, pos)


def moments(rows):
    center = rows - jnp.mean(rows, axis=-1, keepdims=True)
    spread = lax.rsqrt(jnp.mean(center * center, axis=-1, keepdims=True) + 1e-05)
    return center * spread, spread


def norm_back(grad, gain, unit, spread):
    scaled = grad * gain
    return spread * (
        scaled - jnp.mean(scaled, axis=-1, keepdims=True) - unit * jnp.mean(scaled * unit, axis=-1, keepdims=True)
    )


def middle(
    mixed_ref, tok_any, og_any, norm_ref, wout_ref, gu_any, down_any,
    act_ref, done_ref, datt_ref, dheads, sgate_ref, sdown_ref, up_ref, gn_ref,
    mix_in, wffn, rows_in, drow_in, gelu_a, gelu_b, gated, dgate, dup,
    part, part_in, part2, part2_in, gff, ffn_sib, ffn_sum, ffn_in, hid, unit_one, held, held_two, head_out,
    wf_ref, tok_ref, og_ref, part_relay, part2_relay, sems, lsem,
):
    b = lax.axis_index("blk")
    z = lax.axis_index("head")
    chip, core = b // 2, b % 2
    sib = (chip * 2 + 1 - core, z)
    near = [(chip ^ r) * 2 + core for r in (0, 1, 2, 3)]
    flat = [(n, z) for n in near]
    line = [(b, z ^ r) for r in (0, 1, 2, 3)]
    f32, bf16 = jnp.float32, jnp.bfloat16
    own = [
        pltpu.make_async_copy(gu_any, wf_ref.at[0:2], lsem.at[0]),
        pltpu.make_async_copy(down_any, wf_ref.at[2], lsem.at[1]),
        pltpu.make_async_copy(tok_any, tok_ref, lsem.at[2]),
        pltpu.make_async_copy(og_any, og_ref, lsem.at[3]),
    ]
    for c in own:
        c.start()
    greet([sib] + flat[1:] + line[1:])
    go = Sender(sems)
    mid = (z == 1) | (z == 2)
    ends = (z == 0) | (z == 3)

    HALF = 64

    @pl.when(ends)
    def _():
        for h in range(2):
            part_in[h, 2] = jnp.zeros((HALF, 768), bf16)
            part2_in[h, 2] = jnp.zeros((HALF, 768), bf16)

    def scatter(out, arrived, relay, terms, h):
        passed = go(out.at[h, z ^ 3], relay.at[h], line[1], only=ends)
        three = go(out.at[h, z ^ 3], arrived.at[h, 2], line[3], only=mid)
        one = go(out.at[h, z ^ 1], arrived.at[h, 0], line[1])

        @pl.when(mid)
        def _():
            passed.wait_recv()
            out[h, z ^ 2] = (terms[h, z ^ 2] + relay[h].astype(f32)).astype(bf16)

        two = go(out.at[h, z ^ 2], arrived.at[h, 1], line[2])
        return one, two, three

    def gathered(copies):
        copies[0].wait_recv()
        copies[1].wait_recv()
        pl.when(mid)(copies[2].wait_recv)

    mix_c = []
    for h in range(2):
        rows = pl.ds(HALF * h, HALF)
        mix_c.append([go(mixed_ref.at[z ^ r, rows], mix_in.at[h, z], line[r]) for r in (3, 2, 1)])
    for c in own:
        c.wait()
    mine = pltpu.make_async_copy(wf_ref, wffn.at[:, b], lsem.at[0])
    mine.start()
    wf_p = [[go(wf_ref.at[t], wffn.at[t, b], flat[r]) for r in (3, 1, 2)] for t in range(3)]
    wf_s = [go(wf_ref, wffn.at[:, b], sib)]
    mine.wait()

    spreads = []
    row_c = []
    for h in range(2):
        rows = pl.ds(HALF * h, HALF)
        mix_in[h, z] = mixed_ref[z, rows, :]
        for c in mix_c[h]:
            c.wait_recv()
        attn = dot_nt(mix_in[h, 0], wout_ref[0])
        for j in (1, 2, 3):
            attn = attn + dot_nt(mix_in[h, j], wout_ref[j])
        unit, spread = moments(tok_ref[rows, :].astype(f32) + attn)
        hidden = unit * norm_ref[0:1, :] + norm_ref[1:2, :]
        unit_one[h] = unit
        spreads.append(spread)
        hid[h] = hidden
        rows_in[h, z] = hidden.astype(bf16)
        row_c.append(Spread(go, mid, lambda j, h=h: rows_in.at[h, j], z, line))
    row_c[0].pass_on()
    row_c[1].pass_on()
    for t in range(3):
        for k, r in enumerate((3, 1, 2)):
            wf_p[t][k].wait_recv()
            wf_s.append(go(wffn.at[t, near[r]], wffn.at[t, near[r]], sib))
    for c in wf_s:
        c.wait_recv()

    def weight(t):
        return wffn[t].reshape(768, 768)

    part_c = []
    for h in range(2):
        row_c[h].one.wait_recv()
        row_c[h].three.wait_recv()
        rows = rows_in[h].reshape(4 * HALF, 768)
        gate = jnp.dot(rows, weight(0), preferred_element_type=f32)
        up = jnp.dot(rows, weight(1), preferred_element_type=f32)
        half = 0.5 + 0.5 * lax.erf(gate * (0.5**0.5))
        value = gate * half
        slope = half + gate * jnp.exp(-0.5 * gate * gate) * 0.3989422804014327
        gelu_a[h] = slope * up
        gelu_b[h] = value
        low = (value * up).astype(bf16)
        gated[h] = low
        term = dot_nt(low, weight(2)).reshape(4, HALF, 768)
        held[h] = term
        part[h] = term.astype(bf16)
        part_c.append(scatter(part, part_in, part_relay, held, h))
    gains = []
    drow_c = []
    for h in range(2):
        rows = pl.ds(HALF * h, HALF)
        gathered(part_c[h])
        branch = held[h, z] + part_in[h, 0].astype(f32) + part_in[h, 1].astype(f32) + part_in[h, 2].astype(f32)
        unit_two, spread_two = moments(hid[h] + branch)
        grad = og_ref[rows, :].astype(f32)
        d_two = norm_back(grad, norm_ref[2:3, :], unit_two, spread_two)
        hid[h] = d_two
        drow_in[h, z] = d_two.astype(bf16)
        drow_c.append(Spread(go, mid, lambda j, h=h: drow_in.at[h, j], z, line))
        act_ref[rows, :] = (unit_two * norm_ref[2:3, :] + norm_ref[3:4, :]).astype(bf16)
        gains.append((jnp.sum(grad * unit_two, axis=0, keepdims=True), jnp.sum(grad, axis=0, keepdims=True)))
    gn_ref[...] = jnp.zeros((32, 768), f32)
    gn_ref[16:17, :] = gains[0][0] + gains[1][0]
    gn_ref[24:25, :] = gains[0][1] + gains[1][1]
    part2_c = []
    for h in range(2):
        drow_c[h].pass_on()
        drow_c[h].one.wait_recv()
        drow_c[h].three.wait_recv()
        d_gated = jnp.dot(drow_in[h].reshape(4 * HALF, 768), weight(2), preferred_element_type=f32)
        dg = (d_gated * gelu_a[h]).astype(bf16)
        du = (d_gated * gelu_b[h]).astype(bf16)
        dgate[h] = dg
        dup[h] = du
        term = (dot_nt(dg, weight(0)) + dot_nt(du, weight(1))).reshape(4, HALF, 768)
        held_two[h] = term
        part2[h] = term.astype(bf16)
        part2_c.append(scatter(part2, part2_in, part2_relay, held_two, h))
    sib_c = []
    acts = rows_in[...].reshape(512, 768)
    for t in (2, 0, 1):
        if t == 2:
            total = dot_tn(drow_in[...].reshape(512, 768), gated[...].reshape(512, 768))
        else:
            total = dot_tn(acts, (dgate, dup)[t][...].reshape(512, 768))
        gff[t] = total.astype(bf16).reshape(4, 2, 96, 768)
        sib_c.append(go(gff.at[t, :, 1 - core], ffn_sib.at[t], sib))
    ffn_c = []
    for k, t in enumerate((2, 0, 1)):
        sib_c[k].wait_recv()
        for r in (3, 1, 2, 0):
            both = (gff[t, chip ^ r, core].astype(f32) + ffn_sib[t, chip ^ r].astype(f32)).astype(bf16)
            if t == 1:
                up_ref[r] = both
                continue
            ffn_sum[t, r] = both
            if r:
                ffn_c.append(go(ffn_sum.at[t, r], ffn_in.at[t, r - 1], flat[r]))
    gains = []
    head_c = []
    for h in range(2):
        rows = pl.ds(HALF * h, HALF)
        gathered(part2_c[h])
        d_hidden = (
            hid[h] + held_two[h, z]
            + part2_in[h, 0].astype(f32) + part2_in[h, 1].astype(f32) + part2_in[h, 2].astype(f32)
        )
        unit = unit_one[h]
        d_one = norm_back(d_hidden, norm_ref[0:1, :], unit, spreads[h])
        low_one = d_one.astype(bf16)
        for r in (3, 2, 1, 0):
            term = jnp.dot(low_one, wout_ref[z ^ r], preferred_element_type=f32).astype(bf16)
            if r:
                head_out[h, r - 1] = term
                head_c.append(go(head_out.at[h, r - 1], dheads.at[z, rows], line[r]))
            else:
                dheads[z, rows, :] = term
        done_ref[rows, :] = d_one
        datt_ref[rows, :] = low_one
        gains.append((jnp.sum(d_hidden * unit, axis=0, keepdims=True), jnp.sum(d_hidden, axis=0, keepdims=True)))
    gn_ref[0:1, :] = gains[0][0] + gains[1][0]
    gn_ref[8:9, :] = gains[0][1] + gains[1][1]
    for c in ffn_c:
        c.wait_recv()
    for t, ref in ((2, sdown_ref), (0, sgate_ref)):
        ref[...] = (
            ffn_sum[t, 0].astype(f32) + ffn_in[t, 0].astype(f32) + ffn_in[t, 1].astype(f32) + ffn_in[t, 2].astype(f32)
        )
    for c in head_c:
        c.wait_recv()
    go.finish()


def run_middle(mixed, tok, og, norms, wout, gu, down):
    f32, bf16 = jnp.float32, jnp.bfloat16
    S = jax.ShapeDtypeStruct
    V = pltpu.VMEM
    halves = (2, 256, 768)
    return pl.pallas_call(
        middle,
        out_shape=(
            S((128, 768), bf16), S((128, 768), f32), S((128, 768), bf16), S((4, 128, 256), bf16),
            S((96, 768), f32), S((96, 768), f32), S((4, 96, 768), bf16), S((32, 768), f32),
        ),
        in_specs=[VM, HBM, HBM, VM, VM, HBM, HBM],
        out_specs=(VM,) * 8,
        scratch_shapes=[
            V((2, 4, 64, 256), bf16), V((3, 8, 96, 768), bf16), V((2, 4, 64, 768), bf16), V((2, 4, 64, 768), bf16),
            V(halves, f32), V(halves, f32), V(halves, bf16), V(halves, bf16), V(halves, bf16),
            V((2, 4, 64, 768), bf16), V((2, 3, 64, 768), bf16), V((2, 4, 64, 768), bf16), V((2, 3, 64, 768), bf16),
            V((3, 4, 2, 96, 768), bf16), V((3, 4, 96, 768), bf16), V((3, 4, 96, 768), bf16), V((3, 3, 96, 768), bf16),
            V((2, 64, 768), f32), V((2, 64, 768), f32), V((2, 4, 64, 768), f32), V((2, 4, 64, 768), f32),
            V((2, 3, 64, 256), bf16),
            V((3, 96, 768), bf16), V((128, 768), bf16), V((128, 768), bf16), V((2, 64, 768), bf16), V((2, 64, 768), bf16),
            pltpu.SemaphoreType.DMA((2, 84)), pltpu.SemaphoreType.DMA((4,)),
        ],
        compiler_params=pltpu.CompilerParams(
            collective_id=3, has_side_effects=True, vmem_limit_bytes=36 << 20
        ),
        name="middle",
    )(mixed, tok, og, norms, wout, gu, down)


def deliver(*refs):
    dx, sgate, sup, sqkv, sout = refs[:5]
    o_dx, o_gu, o_qkv, o_out, sem = refs[5:]
    pairs = ((dx, o_dx), (sgate, o_gu.at[0]), (sup, o_gu.at[1]), (sqkv, o_qkv), (sout, o_out))
    copies = [pltpu.make_async_copy(s, d, sem.at[i]) for i, (s, d) in enumerate(pairs)]
    for c in copies:
        c.start()
    for c in copies:
        c.wait()


def run_deliver(*arrays):
    f32 = jnp.float32
    S = jax.ShapeDtypeStruct
    return pl.pallas_call(
        deliver,
        out_shape=(S((128, 768), f32), S((2, 96, 768), f32), S((96, 576), f32), S((192, 96), f32)),
        in_specs=[ANY] * 5,
        out_specs=(ANY,) * 4,
        scratch_shapes=[pltpu.SemaphoreType.DMA((5,))],
        compiler_params=pltpu.CompilerParams(vmem_limit_bytes=1 << 20),
        name="deliver",
    )(*arrays)


PACK = (1, 4, 2, 5, 7, 8, 0, 3, 6, 9)


def fast_shards(
    tokens, w_qkv, w_out, w_gate_up, w_down, norm_params, alibi_slope, lengths, placement, out_grad
):
    heads_n = lax.axis_size("head")
    blk_n = lax.axis_size("blk")
    head_idx = lax.axis_index("head")
    blk_idx = lax.axis_index("blk")
    tok_rows, width = tokens.shape
    per_dev = HEADS // heads_n
    group_rows = heads_n * tok_rows
    devs = heads_n * blk_n
    share = w_qkv.shape[0]
    bf16 = jnp.bfloat16

    group_tokens, attn_w, q, kv, wout, norms, kcode, qcode = run_collect(
        lengths, tokens, w_qkv, w_out, norm_params.reshape(1, share), placement.reshape(devs, tok_rows)
    )
    mixed, lse = run_attend(lengths, alibi_slope, q, kv, kcode, qcode)
    act, d_one, d_attn, d_heads, s_gate, s_down, up_sum, g_norm = run_middle(
        mixed, tokens, out_grad, norms, wout.reshape(heads_n, width, 256), w_gate_up, w_down.T
    )
    d_q, dkv, result, s_down = run_attend_back(
        lengths, alibi_slope, q, kv, kcode, qcode, mixed, d_heads, lse, act, s_down
    )
    input_grad, s_qkv, s_out, s_norm, s_up = run_finish(
        dkv.reshape(blk_n, group_rows, 384), d_q.reshape(group_rows, 256),
        group_tokens.reshape(group_rows, width), attn_w.reshape(width, 640),
        d_attn, mixed.reshape(group_rows, 256), d_one, g_norm, up_sum,
    )
    input_grad, s_gu, s_qkv, s_out = run_deliver(input_grad, s_gate, s_up, s_qkv, s_out)
    return (
        result,
        input_grad,
        s_qkv,
        s_out,
        s_gu,
        s_down.T,
        s_norm[0, :share].reshape(share, 1),
    )


def solution(mesh):
    placed = (
        P(("blk", "head"), None),
        P("blk", "head"),
        P("head", "blk"),
        P(None, "blk", "head"),
        P("head", "blk"),
        P("blk", "head"),
        P(),
        P(),
        P(),
        P(("blk", "head"), None),
    )
    small = mesh.shape["blk"] == 8 and mesh.shape["head"] == 4
    return jax.shard_map(
        fast_shards if small else shards,
        mesh=mesh,
        in_specs=placed,
        out_specs=(
            P(("blk", "head"), None),
            P(("blk", "head"), None),
            P("blk", "head"),
            P("head", "blk"),
            P(None, "blk", "head"),
            P("head", "blk"),
            P("blk", "head"),
        ),
        check_vma=False,
    )
```

profile of v0, /device:TPU:0, one launch (start us, length us, event | category | flops | bytes accessed | tf_op | source)
XLA Modules:
  0.0 216.2 jit_solution(18341576522651792968)
XLA Ops:
  0.6 0.0 copy-start
  0.6 0.9 copy-done
  1.6 0.0 copy-start.5
  1.6 0.9 copy-done.5
  2.5 0.0 copy-start.6
  2.5 0.8 copy-done.6
  3.3 0.0 copy-start.7
  3.3 0.7 copy-done.7
  4.0 0.0 copy-start.8
  4.0 0.7 copy-done.8
  4.6 0.0 copy-start.12
  4.6 0.7 copy-done.12
  5.3 0.0 copy-start.1
  5.3 0.0 copy-start.2
  5.3 0.0 copy-start.3
  5.3 0.0 copy-start.4
  5.3 46.0 %collect.1 = (bf16[4,128,768]{2,1,0:T(8,128)(2,1)S(1)}, bf16[8,96,640]{2,1,0:T(8,128)(2,1)S(1)}, bf16[4,128,256]{2,1,0:T(8,128)(2,1)S(1)}, bf16[32,128,384]{2,1,...) custom-call(s32[8]{0:T(128)S(1)} %copy-done.8, ...), custom_call_target="tpu_custom_call" | custom-call | tf_op jit(solution)/shard_map/collect/pallas_call | solution.py:824
  51.3 0.0 copy-start.10
  51.3 0.6 copy-done.10
  51.9 0.0 copy-start.9
  51.9 0.0 copy-start.11
  51.9 15.1 %attend.1 = (bf16[4,128,256]{2,1,0:T(8,128)(2,1)S(1)}, f32[4,8,128]{2,1,0:T(8,128)S(1)}) custom-call(s32[8]{0:T(128)S(1)} %copy-done.8, f32[12]{0:T(128)S(1)} %copy-done.10, bf16[4,128,256]{2,1,0:T(8,128)(2,1)S(1)} %get-tuple-element.38.q_ref, bf16[32,128,384]{2,1,0:T(8,128)(2,1)S(1)} %get-tuple-element.39.kv_ref, ...), custom_call_target="tpu_custom_call" | custom-call | tf_op jit(solution)/shard_map/attend/pallas_call | solution.py:446
  67.0 0.0 copy-done.1
  67.0 0.0 copy-done.2
  67.0 0.0 copy-done.3
  67.0 0.0 copy-done.4
  67.1 83.9 %middle.1 = (bf16[128,768]{1,0:T(8,128)(2,1)S(1)}, f32[128,768]{1,0:T(8,128)S(1)}, bf16[128,768]{1,0:T(8,128)(2,1)S(1)}, bf16[4,128,256]{2,1,0:T(8,128)(2,1)S(1)...) custom-call(bf16[4,128,256]{2,1,0:T(8,128)(2,1)S(1)} %get-tuple-eleme, ...), custom_call_target="tpu_custom_call" | custom-call | tf_op jit(solution)/shard_map/middle/pallas_call | solution.py:1061
  151.0 0.0 copy-done.9
  151.0 0.0 copy-done.11
  151.0 22.5 %attend_back.1 = (bf16[4,128,256]{2,1,0:T(8,128)(2,1)S(1)}, bf16[32,128,384]{2,1,0:T(8,128)(2,1)S(1)}, bf16[128,768]{1,0:T(8,128)(2,1)}, f32[96,768]{1,0:T(8,128)}) custom-call(s32[8]{0:T(128)S(1)} %copy-done.9, f32[12]{0:T(128)S(1)} %copy-done.11, bf16[4,128,256]{2,1,0:T(8,128)(2,1)S(1)} %get-tuple-element.38.q_ref, ...), custom_call_target="tpu_custom_call" | custom-call | tf_op jit(solution)/shard_map/attend_back/pallas_call | solution.py:463
  173.5 41.0 %finish.1 = (f32[128,768]{1,0:T(8,128)S(1)}, f32[96,576]{1,0:T(8,128)S(1)}, f32[192,96]{1,0:T(8,128)S(1)}, f32[8,128]{1,0:T(8,128)S(1)}, f32[96,768]{1,0:T(8,128)S(1)}) custom-call(bf16[8,512,384]{2,1,0:T(8,128)(2,1)S(1)} %bitcast.12, bf16[512,256]{1,0:T(8,128)(2,1)S(1)} %bitcast.17, bf16[512,768]{1,0:T(8,128)(2,1)S(1)} %bitcast.16, ...), custom_call_target="tpu_custom_call" | custom-call | tf_op jit(solution)/shard_map/finish/pallas_call | solution.py:682
  214.5 1.1 deliver.1
  215.6 0.5 slice_bitcast_fusion
Async XLA Ops:
  0.6 0.9 copy-start
  1.6 0.9 copy-start.5
  2.5 0.8 copy-start.6
  3.3 0.7 copy-start.7
  4.0 0.7 copy-start.8
  4.6 0.7 copy-start.12
  5.3 61.7 %copy-start.1 = (bf16[128,768]{1,0:T(8,128)(2,1)S(1)}, bf16[128,768]{1,0:T(8,128)(2,1)}, u32[]{:S(2)}) copy-start(bf16[128,768]{1,0:T(8,128)(2,1)} %tok_any.3) | copy-start | bytes 589828
  5.3 61.7 %copy-start.2 = (bf16[2,96,768]{2,1,0:T(8,128)(2,1)S(1)}, bf16[2,96,768]{2,1,0:T(8,128)(2,1)}, u32[]{:S(2)}) copy-start(bf16[2,96,768]{2,1,0:T(8,128)(2,1)} %gu_any.1) | copy-start | bytes 884740
  5.3 61.7 %copy-start.3 = (bf16[128,768]{1,0:T(8,128)(2,1)S(1)}, bf16[128,768]{1,0:T(8,128)(2,1)}, u32[]{:S(2)}) copy-start(bf16[128,768]{1,0:T(8,128)(2,1)} %og_any.1) | copy-start | bytes 589828
  5.3 61.7 %copy-start.4 = (bf16[768,96]{0,1:T(8,128)(2,1)S(1)}, bf16[768,96]{0,1:T(8,128)(2,1)}, u32[]{:S(2)}) copy-start(bf16[768,96]{0,1:T(8,128)(2,1)} %param.14) | copy-start | bytes 442372
  51.3 0.7 copy-start.10
  51.9 99.0 %copy-start.9 = (s32[8]{0:T(128)S(1)}, s32[8]{0:T(128)}, u32[]{:S(2)}) copy-start(s32[8]{0:T(128)} %len_ref.3) | copy-start | bytes 100
  51.9 99.1 %copy-start.11 = (f32[12]{0:T(128)S(1)}, f32[12]{0:T(128)}, u32[]{:S(2)}) copy-start(f32[12]{0:T(128)} %slope_ref.3) | copy-start | bytes 148
where the time goes:
time: 216 us
  Pallas kernels  210 us (97%)
  local copies, waits for them, and re-layouts  5.83 us (3%)
    pallas_call x1, Pallas kernels, run_middle(): pl.pallas_call(middle, out_shape=(S((128, 768), bf16), S((128, 768), f32)...  83.9 us
    pallas_call x1, Pallas kernels, run_collect(): pl.pallas_call(collect, out_shape=(S((4, 128, 768), bf16), S((8, 96, 640)...  46 us
    pallas_call x1, Pallas kernels, run_finish(): pl.pallas_call(finish, out_shape=(jax.ShapeDtypeStruct((128, 768), f32),...  41 us
    pallas_call x1, Pallas kernels, run_attend_back(): pl.pallas_call(attend_back, out_shape=(jax.ShapeDtypeStruct((heads_n, slo...  22.5 us
    pallas_call x1, Pallas kernels, run_attend(): pl.pallas_call(attend, out_shape=(jax.ShapeDtypeStruct((heads_n, slots, 2...  15.1 us
    unnamed x26, local copies, waits for them, and re-layouts  5.32 us

commit v1 on v0

--- a/solution.py
+++ b/solution.py
@@ -279,6 +279,13 @@
     return jnp.concatenate(parts, axis=0).astype(jnp.bfloat16)
 
 
+def by_head_turned(rows, lanes):
+    turned = rows.T
+    lane = lax.broadcasted_iota(jnp.int32, turned.shape, 0)
+    parts = [jnp.where((lane >= first) & (lane < first + HEAD_DIM), turned, 0.0) for first in lanes]
+    return jnp.concatenate(parts, axis=1).astype(jnp.bfloat16)
+
+
 def key_tiles(kv_ref, j):
     rows = kv_ref.shape[0] * K_SLOTS
     blk = kv_ref[:, pl.ds(pl.multiple_of(j * K_SLOTS, K_SLOTS), K_SLOTS), :]
@@ -298,8 +305,14 @@
     return low // step, (high + step - 1) // step
 
 
-def attend(len_ref, slope_ref, q_ref, kv_ref, kcode_ref, qcode_ref, out_ref, lse_ref, vt_ref):
+def attend(len_any, slope_any, q_ref, kv_ref, kcode_ref, qcode_ref, out_ref, lse_ref, vt_ref, len_ref, slope_ref, few):
     z = lax.axis_index("head")
+    scalars = [
+        pltpu.make_async_copy(len_any, len_ref, few.at[0]),
+        pltpu.make_async_copy(slope_any, slope_ref, few.at[1]),
+    ]
+    for c in scalars:
+        c.start()
     devs, slots, _ = kv_ref.shape
     rows = devs * K_SLOTS
     q_rows = q_ref.shape[0] * Q_SLOTS
@@ -310,21 +323,23 @@
         return 0
 
     lax.fori_loop(0, slots // K_SLOTS, turn, 0)
+    for c in scalars:
+        c.wait()
 
     def chunk(i, _):
         first = pl.multiple_of(i * Q_SLOTS, Q_SLOTS)
         q = q_ref[:, pl.ds(first, Q_SLOTS), :].reshape(q_rows, 256).astype(jnp.float32)
-        qbd = by_head(q, (0, 64, 128))
+        qbt = by_head_turned(q, (0, 64, 128))
         qcode = qcode_ref[i, 0:1, :]
         lo, hi = key_span(len_ref, i, devs)
 
         def block(j, state):
             kv = key_tiles(kv_ref, j)
             keys = jnp.concatenate([kv[:, 0:128], kv[:, 256:384]], axis=1)
-            s_all = lax.dot_general(keys, qbd, (((1,), (1,)), ((), ())), preferred_element_type=jnp.float32)
+            s_all = jnp.dot(keys, qbt, preferred_element_type=jnp.float32)
             dist = jnp.abs(key_tiles(kcode_ref, j) - qcode)
             keep = dist < FAR
-            fresh = []
+            fresh, ps = [], []
             for h in range(3):
                 best, total, acc = state[h]
                 s = jnp.where(keep, s_all[:, 128 * h : 128 * h + 128] - slope_ref[3 * z + h] * dist, masked_score)
@@ -332,9 +347,12 @@
                 factor = jnp.exp(best - top)
                 p = jnp.exp(s - top)
                 total = total * factor + jnp.sum(p, axis=0, keepdims=True)
-                vt = vt_ref[j, LANE_OF[h] : LANE_OF[h] + 64, :]
-                acc = acc * factor + jnp.dot(vt, p.astype(jnp.bfloat16), preferred_element_type=jnp.float32)
-                fresh.append((top, total, acc))
+                ps.append(p.astype(jnp.bfloat16))
+                fresh.append((top, total, acc * factor))
+            both = jnp.dot(vt_ref[j, 0:128, :], jnp.concatenate(ps[0:2], axis=1), preferred_element_type=jnp.float32)
+            last = jnp.dot(vt_ref[j, 192:256, :], ps[2], preferred_element_type=jnp.float32)
+            new = (both[0:64, 0:128], both[64:128, 128:256], last)
+            fresh = [(top, total, acc + term) for (top, total, acc), term in zip(fresh, new)]
             return tuple(fresh)
 
         start = tuple(
@@ -356,9 +374,15 @@
     lax.fori_loop(0, slots // Q_SLOTS, chunk, 0)
 
 
-def attend_back(len_ref, slope_ref, q_ref, kv_ref, kcode_ref, qcode_ref, out_ref, do_ref, lse_ref, act_any, sdown_any,
-                dq_ref, dkv_ref, act_out, sdown_out, kt_ref, sum_ref, sem):
+def attend_back(len_any, slope_any, q_ref, kv_ref, kcode_ref, qcode_ref, out_ref, do_ref, lse_ref, act_any, sdown_any,
+                dq_ref, dkv_ref, act_out, sdown_out, kt_ref, sum_ref, sem, len_ref, slope_ref, few):
     z = lax.axis_index("head")
+    scalars = [
+        pltpu.make_async_copy(len_any, len_ref, few.at[0]),
+        pltpu.make_async_copy(slope_any, slope_ref, few.at[1]),
+    ]
+    for c in scalars:
+        c.start()
     devs, slots, _ = kv_ref.shape
     rows = devs * K_SLOTS
     q_rows = q_ref.shape[0] * Q_SLOTS
@@ -378,14 +402,18 @@
         return 0
 
     lax.fori_loop(0, slots // K_SLOTS, turn, 0)
+    for c in scalars:
+        c.wait()
 
     def chunk(i, _):
         first = pl.multiple_of(i * Q_SLOTS, Q_SLOTS)
         q = q_ref[:, pl.ds(first, Q_SLOTS), :].reshape(q_rows, 256).astype(jnp.float32)
         qbd = by_head(q, (0, 64, 128))
+        qbt = by_head_turned(q, (0, 64, 128))
         do = do_ref[:, pl.ds(first, Q_SLOTS), :].reshape(q_rows, 256).astype(jnp.float32)
         out = out_ref[:, pl.ds(first, Q_SLOTS), :].reshape(q_rows, 256).astype(jnp.float32)
         dobd = by_head(do, LANE_OF)
+        dobt = by_head_turned(do, LANE_OF)
         prod = (do * out).T
         delta = [jnp.sum(prod[f : f + 64, :], axis=0, keepdims=True) for f in LANE_OF]
         qcode = qcode_ref[i, 0:1, :]
@@ -395,8 +423,8 @@
             kv = key_tiles(kv_ref, j)
             keys = jnp.concatenate([kv[:, 0:128], kv[:, 256:384]], axis=1)
             vals = kv[:, 128:384]
-            s_all = lax.dot_general(keys, qbd, (((1,), (1,)), ((), ())), preferred_element_type=jnp.float32)
-            dp_all = lax.dot_general(vals, dobd, (((1,), (1,)), ((), ())), preferred_element_type=jnp.float32)
+            s_all = jnp.dot(keys, qbt, preferred_element_type=jnp.float32)
+            dp_all = jnp.dot(vals, dobt, preferred_element_type=jnp.float32)
             dist = jnp.abs(key_tiles(kcode_ref, j) - qcode)
             keep = dist < FAR
             ps, dss, fresh = [], [], []
@@ -406,8 +434,9 @@
                 ds = (p * (dp_all[:, 128 * h : 128 * h + 128] - delta[h])).astype(jnp.bfloat16)
                 ps.append(p.astype(jnp.bfloat16))
                 dss.append(ds)
-                kt = kt_ref[j, 64 * h : 64 * h + 64, :]
-                fresh.append(state[h] + jnp.dot(kt, ds, preferred_element_type=jnp.float32))
+            both = jnp.dot(kt_ref[j, 0:128, :], jnp.concatenate(dss[0:2], axis=1), preferred_element_type=jnp.float32)
+            last = jnp.dot(kt_ref[j, 128:192, :], dss[2], preferred_element_type=jnp.float32)
+            fresh = [state[0] + both[0:64, 0:128], state[1] + both[64:128, 128:256], state[2] + last]
             dv = jnp.dot(jnp.concatenate(ps, axis=1), dobd, preferred_element_type=jnp.float32)
             dk = jnp.dot(jnp.concatenate(dss, axis=1), qbd, preferred_element_type=jnp.float32)
             sum_ref[j, :, 0:128] += dk[:, 0:128]
@@ -449,9 +478,14 @@
             jax.ShapeDtypeStruct((heads_n, slots, 256), jnp.bfloat16),
             jax.ShapeDtypeStruct((slots // Q_SLOTS, 8, heads_n * Q_SLOTS), jnp.float32),
         ),
-        in_specs=[SM, SM, VM, VM, VM, VM],
+        in_specs=[HBM, HBM, VM, VM, VM, VM],
         out_specs=(VM, VM),
-        scratch_shapes=[pltpu.VMEM((slots // K_SLOTS, 256, devs * K_SLOTS), jnp.bfloat16)],
+        scratch_shapes=[
+            pltpu.VMEM((slots // K_SLOTS, 256, devs * K_SLOTS), jnp.bfloat16),
+            pltpu.SMEM((8,), jnp.int32),
+            pltpu.SMEM((HEADS,), jnp.float32),
+            pltpu.SemaphoreType.DMA((2,)),
+        ],
         compiler_params=pltpu.CompilerParams(vmem_limit_bytes=16 << 20),
         name="attend",
     )(lengths, slopes, q, kv, kcode, qcode)
@@ -468,12 +502,15 @@
             jax.ShapeDtypeStruct(act.shape, act.dtype),
             jax.ShapeDtypeStruct(s_down.shape, s_down.dtype),
         ),
-        in_specs=[SM, SM, VM, VM, VM, VM, VM, VM, VM, ANY, ANY],
+        in_specs=[HBM, HBM, VM, VM, VM, VM, VM, VM, VM, ANY, ANY],
         out_specs=(VM, VM, ANY, ANY),
         scratch_shapes=[
             pltpu.VMEM((slots // K_SLOTS, 256, devs * K_SLOTS), jnp.bfloat16),
             pltpu.VMEM((slots // K_SLOTS, devs * K_SLOTS, 384), jnp.float32),
             pltpu.SemaphoreType.DMA((2,)),
+            pltpu.SMEM((8,), jnp.int32),
+            pltpu.SMEM((HEADS,), jnp.float32),
+            pltpu.SemaphoreType.DMA((2,)),
         ],
         compiler_params=pltpu.CompilerParams(vmem_limit_bytes=26 << 20),
         name="attend_back",
@@ -504,7 +541,7 @@
         self.used = 0
         self.left = []
 
-    def __call__(self, src, dst, peer, only=None, arrive=None):
+    def make(self, src, dst, peer, arrive=None):
         i = self.used
         self.used += 1
         assert i < self.sems.shape[1]
@@ -514,6 +551,9 @@
             device_id=peer, device_id_type=MESH,
         )
         copy.arrive = self.sems.at[1, i]
+        return copy
+
+    def start(self, copy, only=None):
         self.left.append((copy, only))
         if only is None:
             copy.start()
@@ -521,6 +561,17 @@
             pl.when(only)(copy.start)
         return copy
 
+    def __call__(self, src, dst, peer, only=None, arrive=None):
+        return self.start(self.make(src, dst, peer, arrive), only)
+
+    def sent(self, copy):
+        [(_, only)] = [item for item in self.left if item[0] is copy]
+        self.left = [item for item in self.left if item[0] is not copy]
+        if only is None:
+            copy.wait_send()
+        else:
+            pl.when(only)(copy.wait_send)
+
     def finish(self):
         for copy, only in self.left:
             if only is None:
@@ -529,17 +580,52 @@
                 pl.when(only)(copy.wait_send)
 
 
+class Plane:
+    def __init__(self, go, core, slot, me, near, flat, sib):
+        self.go, self.core, self.slot, self.near, self.flat, self.sib = go, core, slot, near, flat, sib
+        self.one = go(slot(me), slot(me), flat[1])
+        self.two = go(slot(me), slot(me), flat[2])
+        self.three = go.make(slot(me), slot(me), flat[3])
+        self.handed = [self.hand(me)]
+
+    def hand(self, n):
+        return self.go(self.slot(n), self.slot(n), self.sib)
+
+    def pass_on(self):
+        for copy, r, turn in ((self.one, 1, 0), (self.two, 2, 1)):
+            copy.wait_recv()
+            block = self.slot(self.near[r])
+            self.go(block, block, self.flat[3 - r], only=self.core == turn, arrive=self.three.arrive)
+            self.handed.append(self.hand(self.near[r]))
+
+    def last(self):
+        self.three.wait_recv()
+        self.handed.append(self.hand(self.near[3]))
+
+    def whole(self):
+        for copy in self.handed:
+            copy.wait_recv()
+
+
 class Spread:
     def __init__(self, go, mid, slot, z, line):
         self.go, self.mid, self.slot, self.z, self.line = go, mid, slot, z, line
         self.two = go(slot(z), slot(z), line[2])
-        self.three = go(slot(z), slot(z), line[3], only=mid)
-        self.one = go(slot(z), slot(z), line[1])
+        self.three = go.make(slot(z), slot(z), line[3])
+        self.one = go.make(slot(z), slot(z), line[1])
+
+    def rest(self):
+        self.go.start(self.three, only=self.mid)
+        self.go.start(self.one)
 
     def pass_on(self):
         self.two.wait_recv()
         far = self.slot(self.z ^ 2)
         self.go(far, far, self.line[1], only=self.mid, arrive=self.three.arrive)
+
+    def wait(self):
+        self.one.wait_recv()
+        self.three.wait_recv()
 
 
 def finish(
@@ -569,6 +655,7 @@
     }
     att[z] = datt_ref[...]
     att_c = Spread(go, mid, lambda j: att.at[j], z, line)
+    att_c.rest()
     nz_c = [go(gn_ref.at[pl.ds((z ^ r) * 8, 8)], nz_in.at[r - 1], line[r]) for r in (1, 2, 3)]
     kv_out = {}
     for q in (3, 2, 1, 0):
@@ -745,17 +832,14 @@
         tile = jnp.concatenate([piece[PACK[2 * k]], piece[PACK[2 * k + 1]]], axis=1)
         wa_ref[:, 128 * k : 128 * k + 128] = tile.astype(bf16)
     wat[b] = wa_ref[...]
-    wout[z, b] = wo_ref[...]
+    wout[z] = wo_ref[...]
     nrm_ref[...] = jnp.zeros((8, 128), f32)
     nrm_ref[0:1, 0:96] = nrm_row[...].astype(f32)
     nr[b, z] = nrm_ref[...]
     greet([sib] + flat[1:] + line[1:])
-    wo_z = [go(wo_ref, wout.at[z, b], line[r]) for r in (3, 2, 1)]
-    nr_z = [go(nrm_ref, nr.at[b, z], line[r]) for r in (3, 2, 1)]
+    tok_z = [Spread(go, mid, lambda j, h=h: gt.at[j, pl.ds(64 * h, 64)], z, line) for h in range(2)]
     wa_p = [go(wa_ref, wat.at[b], flat[r]) for r in (3, 1, 2)]
-    tok_z = Spread(go, mid, lambda j: gt.at[j], z, line)
     wa_s = [go(wa_ref, wat.at[b], sib)]
-    passed = []
     pos = pos_ref[...]
     seq = jnp.zeros(pos.shape, f32)
     end = 0
@@ -772,41 +856,44 @@
     own_code = [code_ref[pl.ds(b * 4 + j, 1), :] for j in range(4)]
     for i in range(4):
         qcode[i, 0:1, :] = jnp.concatenate([c[:, 32 * i : 32 * i + 32] for c in own_code], axis=1)
-    for c in wo_z + nr_z:
-        c.wait_recv()
+    go.sent(tok_z[0].two)
+    tok_z[0].rest()
+    tok_z[0].pass_on()
+    go.sent(tok_z[1].two)
+    tok_z[1].rest()
+    wo_z = [go(wo_ref, wout.at[z], line[r]) for r in (3, 2, 1)]
+    nr_z = [go(nrm_ref, nr.at[b, z], line[r]) for r in (3, 2, 1)]
     for k, r in enumerate((3, 1, 2)):
         wa_p[k].wait_recv()
         wa_s.append(go(wat.at[near[r]], wat.at[near[r]], sib))
-    wo_p = [go(wout.at[:, b], wout.at[:, b], flat[r]) for r in (3, 1, 2)]
-    passed.append(go(wout.at[:, b], wout.at[:, b], sib))
-    nr_p = [go(nr.at[b], nr.at[b], flat[r]) for r in (3, 1, 2)]
-    passed.append(go(nr.at[b], nr.at[b], sib))
+    tok_z[1].pass_on()
     for c in wa_s:
         c.wait_recv()
     kv_p = []
     for r in (0, 2, 1, 3):
-        if r == 2:
-            tok_z.pass_on()
-        elif r:
-            (tok_z.one if r == 1 else tok_z.three).wait_recv()
+        for s in tok_z:
+            if r in (1, 3):
+                (s.one if r == 1 else s.three).wait_recv()
         j = z ^ r
         rows = jnp.dot(gt[j], wat[...].reshape(768, 640), preferred_element_type=f32)
         kv[b * 4 + j] = rows[:, 0:384].astype(bf16)
-        kv_p.append([go(kv.at[b * 4 + j], kv.at[b * 4 + j], flat[s]) for s in (3, 1, 2)])
-        passed.append(go(kv.at[b * 4 + j], kv.at[b * 4 + j], sib))
+        kv_p.append(Plane(go, core, lambda n, j=j: kv.at[n * 4 + j], b, near, flat, sib))
         q_ref[j] = rows[:, 384:640].astype(bf16) * bf16(HEAD_DIM ** (-0.5))
+        if r:
+            kv_p[-2].pass_on()
+        if r == 1:
+            for c in wo_z + nr_z:
+                c.wait_recv()
+            nr_p = [go(nr.at[b], nr.at[b], flat[r]) for r in (3, 1, 2)]
+            passed = [go(nr.at[b], nr.at[b], sib)]
     for k, r in enumerate((3, 1, 2)):
-        wo_p[k].wait_recv()
         nr_p[k].wait_recv()
-        n = near[r]
-        passed.append(go(wout.at[:, n], wout.at[:, n], sib))
-        passed.append(go(nr.at[n], nr.at[n], sib))
-    for step, r in enumerate((0, 2, 1, 3)):
-        j = z ^ r
-        for k, s in enumerate((3, 1, 2)):
-            kv_p[step][k].wait_recv()
-            n = near[s] * 4 + j
-            passed.append(go(kv.at[n], kv.at[n], sib))
+        passed.append(go(nr.at[near[r]], nr.at[near[r]], sib))
+    kv_p[3].pass_on()
+    for p in kv_p:
+        p.last()
+    for p in kv_p:
+        p.whole()
     for c in passed:
         c.wait_recv()
     total = jnp.zeros((8, 768), f32)
@@ -825,14 +912,14 @@
         collect,
         out_shape=(
             S((4, 128, 768), bf16), S((8, 96, 640), bf16), S((4, 128, 256), bf16), S((32, 128, 384), bf16),
-            S((4, 8, 96, 256), bf16), S((8, 768), f32), S((32, 128, 128), f32), S((4, 8, 128), f32),
+            S((4, 96, 256), bf16), S((8, 768), f32), S((32, 128, 128), f32), S((4, 8, 128), f32),
         ),
         in_specs=[HBM] * 6,
         out_specs=(VM,) * 8,
         scratch_shapes=[
             V((96, 640), bf16), V((96, 256), bf16), V((8, 4, 8, 128), f32), V((32, 128), f32),
             V((96, 576), bf16), V((192, 96), bf16), V((1, 96), bf16), V((32, 128), jnp.int32), V((8, 128), f32),
-            pltpu.SMEM((8,), jnp.int32), pltpu.SemaphoreType.DMA((2, 64)), pltpu.SemaphoreType.DMA((6,)),
+            pltpu.SMEM((8,), jnp.int32), pltpu.SemaphoreType.DMA((2, 80)), pltpu.SemaphoreType.DMA((6,)),
         ],
         compiler_params=pltpu.CompilerParams(
             collective_id=1, has_side_effects=True, vmem_limit_bytes=20 << 20
@@ -855,11 +942,11 @@
 
 
 def middle(
-    mixed_ref, tok_any, og_any, norm_ref, wout_ref, gu_any, down_any,
+    mixed_ref, tok_any, og_any, norm_ref, wo_0, wo_1, wo_2, wo_3, gu_any, down_any,
     act_ref, done_ref, datt_ref, dheads, sgate_ref, sdown_ref, up_ref, gn_ref,
     mix_in, wffn, rows_in, drow_in, gelu_a, gelu_b, gated, dgate, dup,
     part, part_in, part2, part2_in, gff, ffn_sib, ffn_sum, ffn_in, hid, unit_one, held, held_two, head_out,
-    wf_ref, tok_ref, og_ref, part_relay, part2_relay, sems, lsem,
+    wf_ref, tok_ref, og_ref, wout, part_relay, part2_relay, sems, lsem,
 ):
     b = lax.axis_index("blk")
     z = lax.axis_index("head")
@@ -884,30 +971,17 @@
 
     HALF = 64
 
-    @pl.when(ends)
-    def _():
-        for h in range(2):
-            part_in[h, 2] = jnp.zeros((HALF, 768), bf16)
-            part2_in[h, 2] = jnp.zeros((HALF, 768), bf16)
-
     def scatter(out, arrived, relay, terms, h):
-        passed = go(out.at[h, z ^ 3], relay.at[h], line[1], only=ends)
-        three = go(out.at[h, z ^ 3], arrived.at[h, 2], line[3], only=mid)
-        one = go(out.at[h, z ^ 1], arrived.at[h, 0], line[1])
-
-        @pl.when(mid)
-        def _():
-            passed.wait_recv()
-            out[h, z ^ 2] = (terms[h, z ^ 2] + relay[h].astype(f32)).astype(bf16)
-
-        two = go(out.at[h, z ^ 2], arrived.at[h, 1], line[2])
-        return one, two, three
+        return [go(out.at[h, z ^ r], arrived.at[h, r - 1], line[r]) for r in (3, 2, 1)]
 
     def gathered(copies):
-        copies[0].wait_recv()
-        copies[1].wait_recv()
-        pl.when(mid)(copies[2].wait_recv)
-
+        for c in copies:
+            c.wait_recv()
+
+    wo_s = []
+    for r, ref in enumerate((wo_0, wo_1, wo_2, wo_3)):
+        wo_s.append(go(ref, wout.at[:, near[r]], sib))
+        wout[:, near[r]] = ref[...]
     mix_c = []
     for h in range(2):
         rows = pl.ds(HALF * h, HALF)
@@ -916,9 +990,14 @@
         c.wait()
     mine = pltpu.make_async_copy(wf_ref, wffn.at[:, b], lsem.at[0])
     mine.start()
-    wf_p = [[go(wf_ref.at[t], wffn.at[t, b], flat[r]) for r in (3, 1, 2)] for t in range(3)]
-    wf_s = [go(wf_ref, wffn.at[:, b], sib)]
     mine.wait()
+    wf_p = [Plane(go, core, lambda n, t=t: wffn.at[t, n], b, near, flat, sib) for t in range(3)]
+
+    for c in wo_s:
+        c.wait_recv()
+
+    def out_weight(j):
+        return wout[j].reshape(768, 256)
 
     spreads = []
     row_c = []
@@ -927,9 +1006,9 @@
         mix_in[h, z] = mixed_ref[z, rows, :]
         for c in mix_c[h]:
             c.wait_recv()
-        attn = dot_nt(mix_in[h, 0], wout_ref[0])
+        attn = dot_nt(mix_in[h, 0], out_weight(0))
         for j in (1, 2, 3):
-            attn = attn + dot_nt(mix_in[h, j], wout_ref[j])
+            attn = attn + dot_nt(mix_in[h, j], out_weight(j))
         unit, spread = moments(tok_ref[rows, :].astype(f32) + attn)
         hidden = unit * norm_ref[0:1, :] + norm_ref[1:2, :]
         unit_one[h] = unit
@@ -937,22 +1016,24 @@
         hid[h] = hidden
         rows_in[h, z] = hidden.astype(bf16)
         row_c.append(Spread(go, mid, lambda j, h=h: rows_in.at[h, j], z, line))
+        if h == 1:
+            row_c[0].rest()
+        wf_p[h].pass_on()
     row_c[0].pass_on()
+    row_c[1].rest()
+    wf_p[2].pass_on()
     row_c[1].pass_on()
-    for t in range(3):
-        for k, r in enumerate((3, 1, 2)):
-            wf_p[t][k].wait_recv()
-            wf_s.append(go(wffn.at[t, near[r]], wffn.at[t, near[r]], sib))
-    for c in wf_s:
-        c.wait_recv()
+    for p in wf_p:
+        p.last()
+    wf_p[0].whole()
+    wf_p[1].whole()
 
     def weight(t):
         return wffn[t].reshape(768, 768)
 
     part_c = []
     for h in range(2):
-        row_c[h].one.wait_recv()
-        row_c[h].three.wait_recv()
+        row_c[h].wait()
         rows = rows_in[h].reshape(4 * HALF, 768)
         gate = jnp.dot(rows, weight(0), preferred_element_type=f32)
         up = jnp.dot(rows, weight(1), preferred_element_type=f32)
@@ -963,6 +1044,8 @@
         gelu_b[h] = value
         low = (value * up).astype(bf16)
         gated[h] = low
+        if h == 0:
+            wf_p[2].whole()
         term = dot_nt(low, weight(2)).reshape(4, HALF, 768)
         held[h] = term
         part[h] = term.astype(bf16)
@@ -981,14 +1064,14 @@
         drow_c.append(Spread(go, mid, lambda j, h=h: drow_in.at[h, j], z, line))
         act_ref[rows, :] = (unit_two * norm_ref[2:3, :] + norm_ref[3:4, :]).astype(bf16)
         gains.append((jnp.sum(grad * unit_two, axis=0, keepdims=True), jnp.sum(grad, axis=0, keepdims=True)))
+        drow_c[h].rest()
     gn_ref[...] = jnp.zeros((32, 768), f32)
     gn_ref[16:17, :] = gains[0][0] + gains[1][0]
     gn_ref[24:25, :] = gains[0][1] + gains[1][1]
     part2_c = []
     for h in range(2):
         drow_c[h].pass_on()
-        drow_c[h].one.wait_recv()
-        drow_c[h].three.wait_recv()
+        drow_c[h].wait()
         d_gated = jnp.dot(drow_in[h].reshape(4 * HALF, 768), weight(2), preferred_element_type=f32)
         dg = (d_gated * gelu_a[h]).astype(bf16)
         du = (d_gated * gelu_b[h]).astype(bf16)
@@ -1031,7 +1114,7 @@
         d_one = norm_back(d_hidden, norm_ref[0:1, :], unit, spreads[h])
         low_one = d_one.astype(bf16)
         for r in (3, 2, 1, 0):
-            term = jnp.dot(low_one, wout_ref[z ^ r], preferred_element_type=f32).astype(bf16)
+            term = jnp.dot(low_one, out_weight(z ^ r), preferred_element_type=f32).astype(bf16)
             if r:
                 head_out[h, r - 1] = term
                 head_c.append(go(head_out.at[h, r - 1], dheads.at[z, rows], line[r]))
@@ -1053,7 +1136,7 @@
     go.finish()
 
 
-def run_middle(mixed, tok, og, norms, wout, gu, down):
+def run_middle(mixed, tok, og, norms, wo, gu, down):
     f32, bf16 = jnp.float32, jnp.bfloat16
     S = jax.ShapeDtypeStruct
     V = pltpu.VMEM
@@ -1064,7 +1147,7 @@
             S((128, 768), bf16), S((128, 768), f32), S((128, 768), bf16), S((4, 128, 256), bf16),
             S((96, 768), f32), S((96, 768), f32), S((4, 96, 768), bf16), S((32, 768), f32),
         ),
-        in_specs=[VM, HBM, HBM, VM, VM, HBM, HBM],
+        in_specs=[VM, HBM, HBM, VM, VM, VM, VM, VM, HBM, HBM],
         out_specs=(VM,) * 8,
         scratch_shapes=[
             V((2, 4, 64, 256), bf16), V((3, 8, 96, 768), bf16), V((2, 4, 64, 768), bf16), V((2, 4, 64, 768), bf16),
@@ -1073,14 +1156,14 @@
             V((3, 4, 2, 96, 768), bf16), V((3, 4, 96, 768), bf16), V((3, 4, 96, 768), bf16), V((3, 3, 96, 768), bf16),
             V((2, 64, 768), f32), V((2, 64, 768), f32), V((2, 4, 64, 768), f32), V((2, 4, 64, 768), f32),
             V((2, 3, 64, 256), bf16),
-            V((3, 96, 768), bf16), V((128, 768), bf16), V((128, 768), bf16), V((2, 64, 768), bf16), V((2, 64, 768), bf16),
-            pltpu.SemaphoreType.DMA((2, 84)), pltpu.SemaphoreType.DMA((4,)),
+            V((3, 96, 768), bf16), V((128, 768), bf16), V((128, 768), bf16), V((4, 8, 96, 256), bf16), V((2, 64, 768), bf16), V((2, 64, 768), bf16),
+            pltpu.SemaphoreType.DMA((2, 108)), pltpu.SemaphoreType.DMA((4,)),
         ],
         compiler_params=pltpu.CompilerParams(
             collective_id=3, has_side_effects=True, vmem_limit_bytes=36 << 20
         ),
         name="middle",
-    )(mixed, tok, og, norms, wout, gu, down)
+    )(mixed, tok, og, norms, *wo, gu, down)
 
 
 def deliver(*refs):
@@ -1125,15 +1208,18 @@
     share = w_qkv.shape[0]
     bf16 = jnp.bfloat16
 
-    group_tokens, attn_w, q, kv, wout, norms, kcode, qcode = run_collect(
-        lengths, tokens, w_qkv, w_out, norm_params.reshape(1, share), placement.reshape(devs, tok_rows)
-    )
-    mixed, lse = run_attend(lengths, alibi_slope, q, kv, kcode, qcode)
+    held = [
+        pltpu.with_memory_space_constraint(a, pltpu.MemorySpace.HBM)
+        for a in (lengths, alibi_slope, tokens, w_qkv, w_out, norm_params.reshape(1, share), placement.reshape(devs, tok_rows))
+    ]
+    group_tokens, attn_w, q, kv, wo, norms, kcode, qcode = run_collect(held[0], *held[2:])
+    wo = [wo] + [lax.ppermute(wo, "blk", [(i, i ^ (2 * r)) for i in range(blk_n)]) for r in (1, 2, 3)]
+    mixed, lse = run_attend(held[0], held[1], q, kv, kcode, qcode)
     act, d_one, d_attn, d_heads, s_gate, s_down, up_sum, g_norm = run_middle(
-        mixed, tokens, out_grad, norms, wout.reshape(heads_n, width, 256), w_gate_up, w_down.T
+        mixed, tokens, out_grad, norms, wo, w_gate_up, w_down.T
     )
     d_q, dkv, result, s_down = run_attend_back(
-        lengths, alibi_slope, q, kv, kcode, qcode, mixed, d_heads, lse, act, s_down
+        held[0], held[1], q, kv, kcode, qcode, mixed, d_heads, lse, act, s_down
     )
     input_grad, s_qkv, s_out, s_norm, s_up = run_finish(
         dkv.reshape(blk_n, group_rows, 384), d_q.reshape(group_rows, 256),

time: 216 us -> 200 us (0.926)
  Pallas kernels: 210 us -> 196 us
  local copies, waits for them, and re-layouts: 5.83 us -> 0.53 us
  starting transfers between devices: 0 us -> 3.55 us
    pallas_call x1, Pallas kernels: 46 us -> 38.6 us  [run_collect(): pl.pallas_call(collect, out_shape=(S((4, 128, 768), bf16), S((8, 96, 640)...]
    unnamed x26 -> x8, local copies, waits for them, and re-layouts: 5.32 us -> 0.02 us
    pallas_call x1, Pallas kernels: 41 us -> 37.2 us  [run_finish(): pl.pallas_call(finish, out_shape=(jax.ShapeDtypeStruct((128, 768), f32),...]
    ppermute x0 -> x3, starting transfers between devices: none -> 3.55 us  [fast_shards(): lax.ppermute(wo, 'blk', [(i, i ^ 2 * r) for i in range(blk_n)])]
  transfers between devices with their start and end apart: 0 -> 3, of which waited for: 0 -> 0; matrix products, arithmetic and copies ran while one was open for 0% -> 0% of each run, Pallas kernels for 0% -> 7%
where the time goes in v1:
time: 200 us; the launch traced here: 201 us
  Pallas kernels  196 us (98%)
  starting transfers between devices  3.55 us (2%)
    pallas_call x1, Pallas kernels, run_middle(): pl.pallas_call(middle, out_shape=(S((128, 768), bf16), S((128, 768), f32)...  82.4 us
    pallas_call x1, Pallas kernels, run_collect(): pl.pallas_call(collect, out_shape=(S((4, 128, 768), bf16), S((8, 96, 640)...  38.6 us
    pallas_call x1, Pallas kernels, run_finish(): pl.pallas_call(finish, out_shape=(jax.ShapeDtypeStruct((128, 768), f32),...  37.2 us
    pallas_call x1, Pallas kernels, run_attend_back(): pl.pallas_call(attend_back, out_shape=(jax.ShapeDtypeStruct((heads_n, slo...  22.1 us
    pallas_call x1, Pallas kernels, run_attend(): pl.pallas_call(attend, out_shape=(jax.ShapeDtypeStruct((heads_n, slots, 2...  14.3 us
  transfers between devices with their start and end apart: 3, of which 0 were waited for; matrix products, arithmetic and copies ran while one was open for 0% of the time, Pallas kernels for 7%

profile of v1, /device:TPU:0, one launch (start us, length us, event | category | flops | bytes accessed | tf_op | source)
XLA Modules:
  0.0 200.8 jit_solution(6715878905941835200)
XLA Ops:
  0.6 0.0 copy-start
  0.6 0.0 copy-start.2
  0.7 0.0 copy-start.3
  0.7 0.0 copy-start.1
  0.7 38.6 %collect.1 = (bf16[4,128,768]{2,1,0:T(8,128)(2,1)S(1)}, bf16[8,96,640]{2,1,0:T(8,128)(2,1)S(1)}, bf16[4,128,256]{2,1,0:T(8,128)(2,1)S(1)}, bf16[32,128,384]{2,1,...) custom-call(s32[8]{0:T(128)} %len_any.5, ...), custom_call_target="tpu_custom_call" | custom-call | tf_op jit(solution)/shard_map/collect/pallas_call | solution.py:911
  39.3 0.9 collective-permute-start.2
  40.2 0.8 collective-permute-start.1
  41.0 1.9 collective-permute-start
  42.9 14.3 %attend.1 = (bf16[4,128,256]{2,1,0:T(8,128)(2,1)S(1)}, f32[4,8,128]{2,1,0:T(8,128)S(1)}) custom-call(s32[8]{0:T(128)} %len_any.5, f32[12]{0:T(128)} %slope_any.3, bf16[4,128,256]{2,1,0:T(8,128)(2,1)S(1)} %get-tuple-element.38.q_ref, bf16[32,128,384]{2,1,0:T(8,128)(2,1)S(1)} %get-tuple-element.39.kv_ref, f32[32,128,128]{2,1,0:T(8,128)S(1)} %get-tuple-element.40.kcode_ref, ...), custom_call_target="tpu_custom_call" | custom-call | tf_op jit(solution)/shard_map/attend/pallas_call | solution.py:475
  57.2 0.0 collective-permute-done.2.wo_3
  57.2 0.0 collective-permute-done.1.wo_2
  57.2 0.0 collective-permute-done.wo_1
  57.2 0.0 copy-done
  57.2 0.0 copy-done.2
  57.3 0.0 copy-done.3
  57.3 0.0 copy-done.1
  57.3 82.4 %middle.1 = (bf16[128,768]{1,0:T(8,128)(2,1)S(1)}, f32[128,768]{1,0:T(8,128)S(1)}, bf16[128,768]{1,0:T(8,128)(2,1)S(1)}, bf16[4,128,256]{2,1,0:T(8,128)(2,1)S(1)...) custom-call(bf16[4,128,256]{2,1,0:T(8,128)(2,1)S(1)} %get-tuple-eleme, ...), custom_call_target="tpu_custom_call" | custom-call | tf_op jit(solution)/shard_map/middle/pallas_call | solution.py:1144
  139.7 22.1 %attend_back.1 = (bf16[4,128,256]{2,1,0:T(8,128)(2,1)S(1)}, bf16[32,128,384]{2,1,0:T(8,128)(2,1)S(1)}, bf16[128,768]{1,0:T(8,128)(2,1)}, f32[96,768]{1,0:T(8,128)}) custom-call(s32[8]{0:T(128)} %len_any.5, f32[12]{0:T(128)} %slope_any.3, bf16[4,128,256]{2,1,0:T(8,128)(2,1)S(1)} %get-tuple-element.38.q_ref, ...), custom_call_target="tpu_custom_call" | custom-call | tf_op jit(solution)/shard_map/attend_back/pallas_call | solution.py:497
  161.8 37.2 %finish.1 = (f32[128,768]{1,0:T(8,128)S(1)}, f32[96,576]{1,0:T(8,128)S(1)}, f32[192,96]{1,0:T(8,128)S(1)}, f32[8,128]{1,0:T(8,128)S(1)}, f32[96,768]{1,0:T(8,128)S(1)}) custom-call(bf16[8,512,384]{2,1,0:T(8,128)(2,1)S(1)} %bitcast.11, bf16[512,256]{1,0:T(8,128)(2,1)S(1)} %bitcast.15, bf16[512,768]{1,0:T(8,128)(2,1)S(1)} %bitcast.14, ...), custom_call_target="tpu_custom_call" | custom-call | tf_op jit(solution)/shard_map/finish/pallas_call | solution.py:769
  199.0 0.5 slice_bitcast_fusion
  199.5 1.1 deliver.1
Async XLA Ops:
  0.6 56.6 %copy-start = (bf16[128,768]{1,0:T(8,128)(2,1)S(1)}, bf16[128,768]{1,0:T(8,128)(2,1)}, u32[]{:S(2)}) copy-start(bf16[128,768]{1,0:T(8,128)(2,1)} %tok_any.3) | copy-start | bytes 589828
  0.6 56.6 %copy-start.2 = (bf16[128,768]{1,0:T(8,128)(2,1)S(1)}, bf16[128,768]{1,0:T(8,128)(2,1)}, u32[]{:S(2)}) copy-start(bf16[128,768]{1,0:T(8,128)(2,1)} %og_any.1) | copy-start | bytes 589828
  0.7 56.6 %copy-start.3 = (bf16[768,96]{0,1:T(8,128)(2,1)S(1)}, bf16[768,96]{0,1:T(8,128)(2,1)}, u32[]{:S(2)}) copy-start(bf16[768,96]{0,1:T(8,128)(2,1)} %param.14) | copy-start | bytes 442372
  0.7 56.6 %copy-start.1 = (bf16[2,96,768]{2,1,0:T(8,128)(2,1)S(1)}, bf16[2,96,768]{2,1,0:T(8,128)(2,1)}, u32[]{:S(2)}) copy-start(bf16[2,96,768]{2,1,0:T(8,128)(2,1)} %gu_any.1) | copy-start | bytes 884740
  39.3 17.9 %collective-permute-start.2 = (bf16[4,96,256]{2,1,0:T(8,128)(2,1)S(1)}, bf16[4,96,256]{2,1,0:T(8,128)(2,1)S(1)}, u32[]{:S(2)}, u32[]{:S(2)}) collective-permute-start(bf16[4,96,256]{2,1,0:T(8,128)(2,1)S(1)} %get-tuple-element.44.wo_0), channel_id=1, source_target_pairs={{0,24},{4,28},{8,16},{12,20},{16,8},{20,12},{24,0},{28,4},{1,25},{... | collective-permute-start | bytes 589832 | tf_op jit(solution)/shard_map/ppermute | solution.py:1216
  40.2 17.0 %collective-permute-start.1 = (bf16[4,96,256]{2,1,0:T(8,128)(2,1)S(1)}, bf16[4,96,256]{2,1,0:T(8,128)(2,1)S(1)}, u32[]{:S(2)}, u32[]{:S(2)}) collective-permute-start(bf16[4,96,256]{2,1,0:T(8,128)(2,1)S(1)} %get-tuple-element.44.wo_0), channel_id=1, source_target_pairs={{0,16},{4,20},{8,24},{12,28},{16,0},{20,4},{24,8},{28,12},{1,17},{... | collective-permute-start | bytes 589832 | tf_op jit(solution)/shard_map/ppermute | solution.py:1216
  41.0 16.2 %collective-permute-start = (bf16[4,96,256]{2,1,0:T(8,128)(2,1)S(1)}, bf16[4,96,256]{2,1,0:T(8,128)(2,1)S(1)}, u32[]{:S(2)}, u32[]{:S(2)}) collective-permute-start(bf16[4,96,256]{2,1,0:T(8,128)(2,1)S(1)} %get-tuple-element.44.wo_0), channel_id=1, source_target_pairs={{0,8},{4,12},{8,0},{12,4},{16,24},{20,28},{24,16},{28,20},{1,9},{5... | collective-permute-start | bytes 589832 | tf_op jit(solution)/shard_map/ppermute | solution.py:1216

commit v2 on v1

--- a/solution.py
+++ b/solution.py
@@ -374,8 +374,8 @@
     lax.fori_loop(0, slots // Q_SLOTS, chunk, 0)
 
 
-def attend_back(len_any, slope_any, q_ref, kv_ref, kcode_ref, qcode_ref, out_ref, do_ref, lse_ref, act_any, sdown_any,
-                dq_ref, dkv_ref, act_out, sdown_out, kt_ref, sum_ref, sem, len_ref, slope_ref, few):
+def attend_back(len_any, slope_any, q_ref, kv_ref, kcode_ref, qcode_ref, out_ref, do_ref, lse_ref, act_any,
+                dq_ref, dkv_ref, act_out, kt_ref, sum_ref, sem, len_ref, slope_ref, few):
     z = lax.axis_index("head")
     scalars = [
         pltpu.make_async_copy(len_any, len_ref, few.at[0]),
@@ -389,7 +389,6 @@
     scale = HEAD_DIM ** (-0.5)
     along = [
         pltpu.make_async_copy(act_any, act_out, sem.at[0]),
-        pltpu.make_async_copy(sdown_any, sdown_out, sem.at[1]),
     ]
     for c in along:
         c.start()
@@ -491,7 +490,7 @@
     )(lengths, slopes, q, kv, kcode, qcode)
 
 
-def run_attend_back(lengths, slopes, q, kv, kcode, qcode, out, do, lse, act, s_down):
+def run_attend_back(lengths, slopes, q, kv, kcode, qcode, out, do, lse, act):
     heads_n, slots, _ = q.shape
     devs = kv.shape[0]
     return pl.pallas_call(
@@ -500,10 +499,9 @@
             jax.ShapeDtypeStruct((heads_n, slots, 256), jnp.bfloat16),
             jax.ShapeDtypeStruct((devs, slots, 384), jnp.bfloat16),
             jax.ShapeDtypeStruct(act.shape, act.dtype),
-            jax.ShapeDtypeStruct(s_down.shape, s_down.dtype),
         ),
-        in_specs=[HBM, HBM, VM, VM, VM, VM, VM, VM, VM, ANY, ANY],
-        out_specs=(VM, VM, ANY, ANY),
+        in_specs=[HBM, HBM, VM, VM, VM, VM, VM, VM, VM, ANY],
+        out_specs=(VM, VM, ANY),
         scratch_shapes=[
             pltpu.VMEM((slots // K_SLOTS, 256, devs * K_SLOTS), jnp.bfloat16),
             pltpu.VMEM((slots // K_SLOTS, devs * K_SLOTS, 384), jnp.float32),
@@ -514,7 +512,7 @@
         ],
         compiler_params=pltpu.CompilerParams(vmem_limit_bytes=26 << 20),
         name="attend_back",
-    )(lengths, slopes, q, kv, kcode, qcode, out, do, lse, act, s_down)
+    )(lengths, slopes, q, kv, kcode, qcode, out, do, lse, act)
 
 
 MESH = pl.DeviceIdType.MESH
@@ -629,9 +627,9 @@
 
 
 def finish(
-    dkv_ref, dq_ref, tok_ref, w_ref, datt_ref, mixed_ref, done_ref, gn_ref, up_ref,
-    dx_ref, sqkv_ref, sout_ref, snorm_ref, sup_ref,
-    up_in, kv_sib, kv_sum, kv_in, g_one, g_two, g_sib, g_sum, g_in,
+    dkv_ref, dq_ref, tok_ref, w_ref, datt_ref, mixed_ref, done_ref, gn_ref,
+    dx_ref, sqkv_ref, sout_ref, snorm_ref,
+    kv_sib, kv_sum, kv_in, g_one, g_two, g_sib, g_sum, g_in,
     part, part_in, att, dkvq, nz_in, nrow, np_in, relay, sems,
 ):
     b = lax.axis_index("blk")
@@ -672,7 +670,6 @@
         relay[...] = jnp.zeros((128, 768), bf16)
         part_in[2] = jnp.zeros((128, 768), bf16)
 
-    up_c = [go(up_ref.at[r], up_in.at[r - 1], flat[r]) for r in (3, 1, 2)]
 
     def send_half(part_i, grads):
         return [
@@ -743,10 +740,7 @@
     half = go(nrow.at[1], np_in.at[0], sib)
     half.wait_recv()
     full = nrow[1] + np_in[0]
-    snorm_ref[...] = pltpu.roll(full, lax.rem(768 - 96 * b, 768), 1)[:, 0:128]
-    for c in up_c:
-        c.wait_recv()
-    sup_ref[...] = up_ref[0].astype(f32) + up_in[0].astype(f32) + up_in[1].astype(f32) + up_in[2].astype(f32)
+    snorm_ref[...] = pltpu.roll(full, lax.rem(768 - 96 * b, 768), 1)[0:1, 0:96]
     two = settle(1, two_out)
     one = settle(0, one_out)
     piece = [two[:, 64 * i : 64 * i + 64] for i in range(6)]
@@ -763,7 +757,7 @@
     go.finish()
 
 
-def run_finish(dkv, dq, toks, w, datt, mixed, done, gn, up):
+def run_finish(dkv, dq, toks, w, datt, mixed, done, gn):
     f32, bf16 = jnp.float32, jnp.bfloat16
     V = pltpu.VMEM
     return pl.pallas_call(
@@ -772,13 +766,11 @@
             jax.ShapeDtypeStruct((128, 768), f32),
             jax.ShapeDtypeStruct((96, 576), f32),
             jax.ShapeDtypeStruct((192, 96), f32),
-            jax.ShapeDtypeStruct((8, 128), f32),
-            jax.ShapeDtypeStruct((96, 768), f32),
+            jax.ShapeDtypeStruct((1, 96), f32),
         ),
-        in_specs=[VM] * 9,
-        out_specs=(VM,) * 5,
+        in_specs=[VM] * 8,
+        out_specs=(VM,) * 4,
         scratch_shapes=[
-            V((3, 96, 768), bf16),
             V((4, 4, 128, 384), bf16), V((4, 4, 128, 384), bf16), V((4, 3, 128, 384), bf16),
             V((768, 384), bf16), V((768, 384), bf16),
             V((2, 4, 96, 384), bf16), V((2, 4, 96, 384), bf16), V((2, 3, 96, 384), bf16),
@@ -790,7 +782,7 @@
             collective_id=5, has_side_effects=True, vmem_limit_bytes=28 << 20
         ),
         name="finish",
-    )(dkv, dq, toks, w, datt, mixed, done, gn, up)
+    )(dkv, dq, toks, w, datt, mixed, done, gn)
 
 
 def collect(
@@ -877,10 +869,14 @@
         j = z ^ r
         rows = jnp.dot(gt[j], wat[...].reshape(768, 640), preferred_element_type=f32)
         kv[b * 4 + j] = rows[:, 0:384].astype(bf16)
-        kv_p.append(Plane(go, core, lambda n, j=j: kv.at[n * 4 + j], b, near, flat, sib))
+        if r == 3:
+            kv_l = [go(kv.at[b * 4 + j], kv.at[b * 4 + j], flat[s]) for s in (3, 1, 2)]
+            passed.append(go(kv.at[b * 4 + j], kv.at[b * 4 + j], sib))
+        else:
+            kv_p.append(Plane(go, core, lambda n, j=j: kv.at[n * 4 + j], b, near, flat, sib))
         q_ref[j] = rows[:, 384:640].astype(bf16) * bf16(HEAD_DIM ** (-0.5))
         if r:
-            kv_p[-2].pass_on()
+            kv_p[{2: 0, 1: 1, 3: 2}[r]].pass_on()
         if r == 1:
             for c in wo_z + nr_z:
                 c.wait_recv()
@@ -889,9 +885,12 @@
     for k, r in enumerate((3, 1, 2)):
         nr_p[k].wait_recv()
         passed.append(go(nr.at[near[r]], nr.at[near[r]], sib))
-    kv_p[3].pass_on()
     for p in kv_p:
         p.last()
+    for k, s in enumerate((3, 1, 2)):
+        kv_l[k].wait_recv()
+        n = near[s] * 4 + (z ^ 3)
+        passed.append(go(kv.at[n], kv.at[n], sib))
     for p in kv_p:
         p.whole()
     for c in passed:
@@ -943,9 +942,9 @@
 
 def middle(
     mixed_ref, tok_any, og_any, norm_ref, wo_0, wo_1, wo_2, wo_3, gu_any, down_any,
-    act_ref, done_ref, datt_ref, dheads, sgate_ref, sdown_ref, up_ref, gn_ref,
+    act_ref, done_ref, datt_ref, dheads, sum_0, sum_1, sum_2, sum_3, gn_ref,
     mix_in, wffn, rows_in, drow_in, gelu_a, gelu_b, gated, dgate, dup,
-    part, part_in, part2, part2_in, gff, ffn_sib, ffn_sum, ffn_in, hid, unit_one, held, held_two, head_out,
+    part, part_in, part2, part2_in, gff, ffn_sib, hid, unit_one, held, held_two, head_out,
     wf_ref, tok_ref, og_ref, wout, part_relay, part2_relay, sems, lsem,
 ):
     b = lax.axis_index("blk")
@@ -971,12 +970,34 @@
 
     HALF = 64
 
+    @pl.when(ends)
+    def _():
+        for h in range(2):
+            part_in[h, 2] = jnp.zeros((HALF, 768), bf16)
+            part2_in[h, 2] = jnp.zeros((HALF, 768), bf16)
+
     def scatter(out, arrived, relay, terms, h):
-        return [go(out.at[h, z ^ r], arrived.at[h, r - 1], line[r]) for r in (3, 2, 1)]
+        passed = go(out.at[h, z ^ 3], relay.at[h], line[1], only=ends)
+        three = go(out.at[h, z ^ 3], arrived.at[h, 2], line[3], only=mid)
+        one = go(out.at[h, z ^ 1], arrived.at[h, 0], line[1])
+        two = go.make(out.at[h, z ^ 2], arrived.at[h, 1], line[2])
+        go.start(two, only=ends)
+
+        def later():
+            @pl.when(mid)
+            def _():
+                passed.wait_recv()
+                out[h, z ^ 2] = (terms[h, z ^ 2] + relay[h].astype(f32)).astype(bf16)
+
+            go.left.append((two, mid))
+            pl.when(mid)(two.start)
+
+        return one, two, three, later
 
     def gathered(copies):
-        for c in copies:
-            c.wait_recv()
+        copies[0].wait_recv()
+        copies[1].wait_recv()
+        pl.when(mid)(copies[2].wait_recv)
 
     wo_s = []
     for r, ref in enumerate((wo_0, wo_1, wo_2, wo_3)):
@@ -1039,9 +1060,6 @@
         up = jnp.dot(rows, weight(1), preferred_element_type=f32)
         half = 0.5 + 0.5 * lax.erf(gate * (0.5**0.5))
         value = gate * half
-        slope = half + gate * jnp.exp(-0.5 * gate * gate) * 0.3989422804014327
-        gelu_a[h] = slope * up
-        gelu_b[h] = value
         low = (value * up).astype(bf16)
         gated[h] = low
         if h == 0:
@@ -1049,11 +1067,19 @@
         term = dot_nt(low, weight(2)).reshape(4, HALF, 768)
         held[h] = term
         part[h] = term.astype(bf16)
+        if h == 1:
+            part_c[0][3]()
         part_c.append(scatter(part, part_in, part_relay, held, h))
+        slope = half + gate * jnp.exp(-0.5 * gate * gate) * 0.3989422804014327
+        gelu_a[h] = slope * up
+        gelu_b[h] = value
+    part_c[1][3]()
     gains = []
     drow_c = []
     for h in range(2):
         rows = pl.ds(HALF * h, HALF)
+        if h == 1:
+            drow_c[0].pass_on()
         gathered(part_c[h])
         branch = held[h, z] + part_in[h, 0].astype(f32) + part_in[h, 1].astype(f32) + part_in[h, 2].astype(f32)
         unit_two, spread_two = moments(hid[h] + branch)
@@ -1070,7 +1096,8 @@
     gn_ref[24:25, :] = gains[0][1] + gains[1][1]
     part2_c = []
     for h in range(2):
-        drow_c[h].pass_on()
+        if h == 1:
+            drow_c[1].pass_on()
         drow_c[h].wait()
         d_gated = jnp.dot(drow_in[h].reshape(4 * HALF, 768), weight(2), preferred_element_type=f32)
         dg = (d_gated * gelu_a[h]).astype(bf16)
@@ -1080,7 +1107,10 @@
         term = (dot_nt(dg, weight(0)) + dot_nt(du, weight(1))).reshape(4, HALF, 768)
         held_two[h] = term
         part2[h] = term.astype(bf16)
+        if h == 1:
+            part2_c[0][3]()
         part2_c.append(scatter(part2, part2_in, part2_relay, held_two, h))
+    part2_c[1][3]()
     sib_c = []
     acts = rows_in[...].reshape(512, 768)
     for t in (2, 0, 1):
@@ -1090,17 +1120,6 @@
             total = dot_tn(acts, (dgate, dup)[t][...].reshape(512, 768))
         gff[t] = total.astype(bf16).reshape(4, 2, 96, 768)
         sib_c.append(go(gff.at[t, :, 1 - core], ffn_sib.at[t], sib))
-    ffn_c = []
-    for k, t in enumerate((2, 0, 1)):
-        sib_c[k].wait_recv()
-        for r in (3, 1, 2, 0):
-            both = (gff[t, chip ^ r, core].astype(f32) + ffn_sib[t, chip ^ r].astype(f32)).astype(bf16)
-            if t == 1:
-                up_ref[r] = both
-                continue
-            ffn_sum[t, r] = both
-            if r:
-                ffn_c.append(go(ffn_sum.at[t, r], ffn_in.at[t, r - 1], flat[r]))
     gains = []
     head_c = []
     for h in range(2):
@@ -1125,12 +1144,11 @@
         gains.append((jnp.sum(d_hidden * unit, axis=0, keepdims=True), jnp.sum(d_hidden, axis=0, keepdims=True)))
     gn_ref[0:1, :] = gains[0][0] + gains[1][0]
     gn_ref[8:9, :] = gains[0][1] + gains[1][1]
-    for c in ffn_c:
-        c.wait_recv()
-    for t, ref in ((2, sdown_ref), (0, sgate_ref)):
-        ref[...] = (
-            ffn_sum[t, 0].astype(f32) + ffn_in[t, 0].astype(f32) + ffn_in[t, 1].astype(f32) + ffn_in[t, 2].astype(f32)
-        )
+    for k, t in enumerate((2, 0, 1)):
+        sib_c[k].wait_recv()
+        for r, ref in enumerate((sum_0, sum_1, sum_2, sum_3)):
+            both = gff[t, chip ^ r, core].astype(f32) + ffn_sib[t, chip ^ r].astype(f32)
+            ref[t] = both.astype(bf16)
     for c in head_c:
         c.wait_recv()
     go.finish()
@@ -1145,15 +1163,15 @@
         middle,
         out_shape=(
             S((128, 768), bf16), S((128, 768), f32), S((128, 768), bf16), S((4, 128, 256), bf16),
-            S((96, 768), f32), S((96, 768), f32), S((4, 96, 768), bf16), S((32, 768), f32),
+            *[S((3, 96, 768), bf16)] * 4, S((32, 768), f32),
         ),
         in_specs=[VM, HBM, HBM, VM, VM, VM, VM, VM, HBM, HBM],
-        out_specs=(VM,) * 8,
+        out_specs=(VM,) * 9,
         scratch_shapes=[
             V((2, 4, 64, 256), bf16), V((3, 8, 96, 768), bf16), V((2, 4, 64, 768), bf16), V((2, 4, 64, 768), bf16),
             V(halves, f32), V(halves, f32), V(halves, bf16), V(halves, bf16), V(halves, bf16),
             V((2, 4, 64, 768), bf16), V((2, 3, 64, 768), bf16), V((2, 4, 64, 768), bf16), V((2, 3, 64, 768), bf16),
-            V((3, 4, 2, 96, 768), bf16), V((3, 4, 96, 768), bf16), V((3, 4, 96, 768), bf16), V((3, 3, 96, 768), bf16),
+            V((3, 4, 2, 96, 768), bf16), V((3, 4, 96, 768), bf16),
             V((2, 64, 768), f32), V((2, 64, 768), f32), V((2, 4, 64, 768), f32), V((2, 4, 64, 768), f32),
             V((2, 3, 64, 256), bf16),
             V((3, 96, 768), bf16), V((128, 768), bf16), V((128, 768), bf16), V((4, 8, 96, 256), bf16), V((2, 64, 768), bf16), V((2, 64, 768), bf16),
@@ -1167,12 +1185,18 @@
 
 
 def deliver(*refs):
-    dx, sgate, sup, sqkv, sout = refs[:5]
-    o_dx, o_gu, o_qkv, o_out, sem = refs[5:]
-    pairs = ((dx, o_dx), (sgate, o_gu.at[0]), (sup, o_gu.at[1]), (sqkv, o_qkv), (sout, o_out))
+    dx, sqkv, sout, snorm, *sums = refs[:8]
+    o_dx, o_qkv, o_out, o_norm, o_gu, o_down, sem = refs[8:]
+    pairs = ((dx, o_dx), (sqkv, o_qkv), (sout, o_out), (snorm, o_norm))
     copies = [pltpu.make_async_copy(s, d, sem.at[i]) for i, (s, d) in enumerate(pairs)]
     for c in copies:
         c.start()
+    for t in range(3):
+        total = sum(s[t].astype(jnp.float32) for s in sums)
+        if t < 2:
+            o_gu[t] = total
+        else:
+            o_down[...] = total
     for c in copies:
         c.wait()
 
@@ -1182,11 +1206,14 @@
     S = jax.ShapeDtypeStruct
     return pl.pallas_call(
         deliver,
-        out_shape=(S((128, 768), f32), S((2, 96, 768), f32), S((96, 576), f32), S((192, 96), f32)),
-        in_specs=[ANY] * 5,
-        out_specs=(ANY,) * 4,
-        scratch_shapes=[pltpu.SemaphoreType.DMA((5,))],
-        compiler_params=pltpu.CompilerParams(vmem_limit_bytes=1 << 20),
+        out_shape=(
+            S((128, 768), f32), S((96, 576), f32), S((192, 96), f32), S((1, 96), f32),
+            S((2, 96, 768), f32), S((96, 768), f32),
+        ),
+        in_specs=[ANY] * 4 + [VM] * 4,
+        out_specs=(ANY,) * 4 + (VM,) * 2,
+        scratch_shapes=[pltpu.SemaphoreType.DMA((4,))],
+        compiler_params=pltpu.CompilerParams(vmem_limit_bytes=8 << 20),
         name="deliver",
     )(*arrays)
 
@@ -1215,18 +1242,21 @@
     group_tokens, attn_w, q, kv, wo, norms, kcode, qcode = run_collect(held[0], *held[2:])
     wo = [wo] + [lax.ppermute(wo, "blk", [(i, i ^ (2 * r)) for i in range(blk_n)]) for r in (1, 2, 3)]
     mixed, lse = run_attend(held[0], held[1], q, kv, kcode, qcode)
-    act, d_one, d_attn, d_heads, s_gate, s_down, up_sum, g_norm = run_middle(
+    act, d_one, d_attn, d_heads, *sums, g_norm = run_middle(
         mixed, tokens, out_grad, norms, wo, w_gate_up, w_down.T
     )
-    d_q, dkv, result, s_down = run_attend_back(
-        held[0], held[1], q, kv, kcode, qcode, mixed, d_heads, lse, act, s_down
-    )
-    input_grad, s_qkv, s_out, s_norm, s_up = run_finish(
+    sums = [sums[0]] + [
+        lax.ppermute(sums[r], "blk", [(i, i ^ (2 * r)) for i in range(blk_n)]) for r in (1, 2, 3)
+    ]
+    d_q, dkv, result = run_attend_back(
+        held[0], held[1], q, kv, kcode, qcode, mixed, d_heads, lse, act
+    )
+    input_grad, s_qkv, s_out, s_norm = run_finish(
         dkv.reshape(blk_n, group_rows, 384), d_q.reshape(group_rows, 256),
         group_tokens.reshape(group_rows, width), attn_w.reshape(width, 640),
-        d_attn, mixed.reshape(group_rows, 256), d_one, g_norm, up_sum,
-    )
-    input_grad, s_gu, s_qkv, s_out = run_deliver(input_grad, s_gate, s_up, s_qkv, s_out)
+        d_attn, mixed.reshape(group_rows, 256), d_one, g_norm,
+    )
+    input_grad, s_qkv, s_out, s_norm, s_gu, s_down = run_deliver(input_grad, s_qkv, s_out, s_norm, *sums)
     return (
         result,
         input_grad,
@@ -1234,7 +1264,7 @@
         s_out,
         s_gu,
         s_down.T,
-        s_norm[0, :share].reshape(share, 1),
+        s_norm.reshape(share, 1),
     )
 
 

time: 200 us -> 193 us (0.965)
  Pallas kernels: 196 us -> 184 us
  starting transfers between devices: 3.55 us -> 7.25 us
    pallas_call x1, Pallas kernels: 82.4 us -> 75 us  [run_middle(): pl.pallas_call(middle, out_shape=(S((128, 768), bf16), S((128, 768), f32)...]
    ppermute x0 -> x3, starting transfers between devices: none -> 3.55 us  [fast_shards(): lax.ppermute(sums[r], 'blk', [(i, i ^ 2 * r) for i in range(blk_n)])]
  transfers between devices with their start and end apart: 3 -> 6, of which waited for: 0 -> 0; matrix products, arithmetic and copies ran while one was open for 0% -> 0% of each run, Pallas kernels for 7% -> 37%
where the time goes in v2:
time: 193 us; the launch traced here: 192 us
  Pallas kernels  184 us (95%)
  starting transfers between devices  7.25 us (4%)
    pallas_call x1, Pallas kernels, run_middle(): pl.pallas_call(middle, out_shape=(S((128, 768), bf16), S((128, 768), f32)...  75 us
    pallas_call x1, Pallas kernels, run_collect(): pl.pallas_call(collect, out_shape=(S((4, 128, 768), bf16), S((8, 96, 640)...  36.8 us
    pallas_call x1, Pallas kernels, run_finish(): pl.pallas_call(finish, out_shape=(jax.ShapeDtypeStruct((128, 768), f32),...  35.6 us
    pallas_call x1, Pallas kernels, run_attend_back(): pl.pallas_call(attend_back, out_shape=(jax.ShapeDtypeStruct((heads_n, slo...  21.1 us
    pallas_call x1, Pallas kernels, run_attend(): pl.pallas_call(attend, out_shape=(jax.ShapeDtypeStruct((heads_n, slots, 2...  13.7 us
  transfers between devices with their start and end apart: 6, of which 0 were waited for; matrix products, arithmetic and copies ran while one was open for 0% of the time, Pallas kernels for 37%

profile of v2, /device:TPU:0, one launch (start us, length us, event | category | flops | bytes accessed | tf_op | source)
XLA Modules:
  0.0 192.3 jit_solution(14261780648786448624)
XLA Ops:
  0.6 0.0 copy-start
  0.6 0.0 copy-start.2
  0.7 0.0 copy-start.3
  0.7 0.0 copy-start.1
  0.7 36.8 %collect.1 = (bf16[4,128,768]{2,1,0:T(8,128)(2,1)S(1)}, bf16[8,96,640]{2,1,0:T(8,128)(2,1)S(1)}, bf16[4,128,256]{2,1,0:T(8,128)(2,1)S(1)}, bf16[32,128,384]{2,1,...) custom-call(s32[8]{0:T(128)} %len_any.5, ...), custom_call_target="tpu_custom_call" | custom-call | tf_op jit(solution)/shard_map/collect/pallas_call | solution.py:910
  37.5 2.5 %collective-permute-start.2 = (bf16[4,96,256]{2,1,0:T(8,128)(2,1)S(1)}, bf16[4,96,256]{2,1,0:T(8,128)(2,1)S(1)}, u32[]{:S(2)}, u32[]{:S(2)}) collective-permute-start(bf16[4,96,256]{2,1,0:T(8,128)(2,1)S(1)} %get-tuple-element.45.wo_0), channel_id=1, source_target_pairs={{0,24},{4,28},{8,16},{12,20},{16,8},{20,12},{24,0},{28,4},{1,25},{... | collective-permute-start | bytes 589832 | tf_op jit(solution)/shard_map/ppermute | solution.py:1243
  40.0 1.2 collective-permute-start.1
  41.2 0.0 collective-permute-start
  41.2 13.7 %attend.1 = (bf16[4,128,256]{2,1,0:T(8,128)(2,1)S(1)}, f32[4,8,128]{2,1,0:T(8,128)S(1)}) custom-call(s32[8]{0:T(128)} %len_any.5, f32[12]{0:T(128)} %slope_any.3, bf16[4,128,256]{2,1,0:T(8,128)(2,1)S(1)} %get-tuple-element.39.q_ref, bf16[32,128,384]{2,1,0:T(8,128)(2,1)S(1)} %get-tuple-element.40.kv_ref, f32[32,128,128]{2,1,0:T(8,128)S(1)} %get-tuple-element.41.kcode_ref, ...), custom_call_target="tpu_custom_call" | custom-call | tf_op jit(solution)/shard_map/attend/pallas_call | solution.py:474
  54.9 0.0 collective-permute-done.2.wo_3
  54.9 0.0 collective-permute-done.1.wo_2
  54.9 0.0 collective-permute-done.wo_1
  54.9 0.0 copy-done
  54.9 0.0 copy-done.2
  55.0 0.0 copy-done.3
  55.0 0.0 copy-done.1
  55.0 75.0 %middle.1 = (bf16[128,768]{1,0:T(8,128)(2,1)S(1)}, f32[128,768]{1,0:T(8,128)S(1)}, bf16[128,768]{1,0:T(8,128)(2,1)S(1)}, bf16[4,128,256]{2,1,0:T(8,128)(2,1)S(1)...) custom-call(bf16[4,128,256]{2,1,0:T(8,128)(2,1)S(1)} %get-tuple-elem, ...), custom_call_target="tpu_custom_call" | custom-call | tf_op jit(solution)/shard_map/middle/pallas_call | solution.py:1162
  130.0 0.4 collective-permute-start.3
  130.4 2.0 %collective-permute-start.4 = (bf16[3,96,768]{2,1,0:T(8,128)(2,1)S(1)}, bf16[3,96,768]{2,1,0:T(8,128)(2,1)S(1)}, u32[]{:S(2)}, u32[]{:S(2)}) collective-permute-start(bf16[3,96,768]{2,1,0:T(8,128)(2,1)S(1)} %get-tuple-element.63), channel_id=1, source_target_pairs={{0,16},{4,20},{8,24},{12,28},{16,0},{20,4},{24,8},{28,12},{1,17},{... | collective-permute-start | bytes 1327112 | tf_op jit(solution)/shard_map/ppermute | solution.py:1249
  132.4 1.2 collective-permute-start.5
  133.6 21.1 %attend_back.1 = (bf16[4,128,256]{2,1,0:T(8,128)(2,1)S(1)}, bf16[32,128,384]{2,1,0:T(8,128)(2,1)S(1)}, bf16[128,768]{1,0:T(8,128)(2,1)}) custom-call(s32[8]{0:T(128)} %len_any.5, f32[12]{0:T(128)} %slope_any.3, bf16[4,128,256]{2,1,0:T(8,128)(2,1)S(1)} %get-tuple-element.39.q_ref, bf16[32,128,384]{2,1,0:T(8,128)(2,1)S(1)} %get-tuple-element.40.kv_ref, ...), custom_call_target="tpu_custom_call" | custom-call | tf_op jit(solution)/shard_map/attend_back/pallas_call | solution.py:496
  154.7 35.6 %finish.1 = (f32[128,768]{1,0:T(8,128)S(1)}, f32[96,576]{1,0:T(8,128)S(1)}, f32[192,96]{1,0:T(8,128)S(1)}, f32[1,96]{1,0:T(1,128)S(1)}) custom-call(bf16[8,512,384]{2,1,0:T(8,128)(2,1)S(1)} %bitcast.10, bf16[512,256]{1,0:T(8,128)(2,1)S(1)} %bitcast.14, bf16[512,768]{1,0:T(8,128)(2,1)S(1)} %bitcast.13, bf16[768,640]{1,0:T(8,128)(2,1)S(1)} %bitcast.12, ...), custom_call_target="tpu_custom_call" | custom-call | tf_op jit(solution)/shard_map/finish/pallas_call | solution.py:763
  190.3 0.0 collective-permute-done.3.refs_5_
  190.3 0.0 collective-permute-done.4.refs_6_
  190.3 0.0 collective-permute-done.5.refs_7_
  190.3 1.8 deliver.1
Async XLA Ops:
  0.6 54.3 %copy-start = (bf16[128,768]{1,0:T(8,128)(2,1)S(1)}, bf16[128,768]{1,0:T(8,128)(2,1)}, u32[]{:S(2)}) copy-start(bf16[128,768]{1,0:T(8,128)(2,1)} %tok_any.3) | copy-start | bytes 589828
  0.6 54.3 %copy-start.2 = (bf16[128,768]{1,0:T(8,128)(2,1)S(1)}, bf16[128,768]{1,0:T(8,128)(2,1)}, u32[]{:S(2)}) copy-start(bf16[128,768]{1,0:T(8,128)(2,1)} %og_any.1) | copy-start | bytes 589828
  0.7 54.3 %copy-start.3 = (bf16[768,96]{0,1:T(8,128)(2,1)S(1)}, bf16[768,96]{0,1:T(8,128)(2,1)}, u32[]{:S(2)}) copy-start(bf16[768,96]{0,1:T(8,128)(2,1)} %param.14) | copy-start | bytes 442372
  0.7 54.3 %copy-start.1 = (bf16[2,96,768]{2,1,0:T(8,128)(2,1)S(1)}, bf16[2,96,768]{2,1,0:T(8,128)(2,1)}, u32[]{:S(2)}) copy-start(bf16[2,96,768]{2,1,0:T(8,128)(2,1)} %gu_any.1) | copy-start | bytes 884740
  37.5 17.5 %collective-permute-start.2 = (bf16[4,96,256]{2,1,0:T(8,128)(2,1)S(1)}, bf16[4,96,256]{2,1,0:T(8,128)(2,1)S(1)}, u32[]{:S(2)}, u32[]{:S(2)}) collective-permute-start(bf16[4,96,256]{2,1,0:T(8,128)(2,1)S(1)} %get-tuple-element.45.wo_0), channel_id=1, source_target_pairs={{0,24},{4,28},{8,16},{12,20},{16,8},{20,12},{24,0},{28,4},{1,25},{... | collective-permute-start | bytes 589832 | tf_op jit(solution)/shard_map/ppermute | solution.py:1243
  40.0 14.9 %collective-permute-start.1 = (bf16[4,96,256]{2,1,0:T(8,128)(2,1)S(1)}, bf16[4,96,256]{2,1,0:T(8,128)(2,1)S(1)}, u32[]{:S(2)}, u32[]{:S(2)}) collective-permute-start(bf16[4,96,256]{2,1,0:T(8,128)(2,1)S(1)} %get-tuple-element.45.wo_0), channel_id=1, source_target_pairs={{0,16},{4,20},{8,24},{12,28},{16,0},{20,4},{24,8},{28,12},{1,17},{... | collective-permute-start | bytes 589832 | tf_op jit(solution)/shard_map/ppermute | solution.py:1243
  41.2 13.8 %collective-permute-start = (bf16[4,96,256]{2,1,0:T(8,128)(2,1)S(1)}, bf16[4,96,256]{2,1,0:T(8,128)(2,1)S(1)}, u32[]{:S(2)}, u32[]{:S(2)}) collective-permute-start(bf16[4,96,256]{2,1,0:T(8,128)(2,1)S(1)} %get-tuple-element.45.wo_0), channel_id=1, source_target_pairs={{0,8},{4,12},{8,0},{12,4},{16,24},{20,28},{24,16},{28,20},{1,9},{5... | collective-permute-start | bytes 589832 | tf_op jit(solution)/shard_map/ppermute | solution.py:1243
  130.0 60.3 %collective-permute-start.3 = (bf16[3,96,768]{2,1,0:T(8,128)(2,1)S(1)}, bf16[3,96,768]{2,1,0:T(8,128)(2,1)S(1)}, u32[]{:S(2)}, u32[]{:S(2)}) collective-permute-start(bf16[3,96,768]{2,1,0:T(8,128)(2,1)S(1)} %get-tuple-element.62), channel_id=1, source_target_pairs={{0,8},{4,12},{8,0},{12,4},{16,24},{20,28},{24,16},{28,20},{1,9},{5... | collective-permute-start | bytes 1327112 | tf_op jit(solution)/shard_map/ppermute | solution.py:1249
  130.4 59.9 %collective-permute-start.4 = (bf16[3,96,768]{2,1,0:T(8,128)(2,1)S(1)}, bf16[3,96,768]{2,1,0:T(8,128)(2,1)S(1)}, u32[]{:S(2)}, u32[]{:S(2)}) collective-permute-start(bf16[3,96,768]{2,1,0:T(8,128)(2,1)S(1)} %get-tuple-element.63), channel_id=1, source_target_pairs={{0,16},{4,20},{8,24},{12,28},{16,0},{20,4},{24,8},{28,12},{1,17},{... | collective-permute-start | bytes 1327112 | tf_op jit(solution)/shard_map/ppermute | solution.py:1249
  132.4 57.9 %collective-permute-start.5 = (bf16[3,96,768]{2,1,0:T(8,128)(2,1)S(1)}, bf16[3,96,768]{2,1,0:T(8,128)(2,1)S(1)}, u32[]{:S(2)}, u32[]{:S(2)}) collective-permute-start(bf16[3,96,768]{2,1,0:T(8,128)(2,1)S(1)} %get-tuple-element.64), channel_id=1, source_target_pairs={{0,24},{4,28},{8,16},{12,20},{16,8},{20,12},{24,0},{28,4},{1,25},{... | collective-permute-start | bytes 1327112 | tf_op jit(solution)/shard_map/ppermute | solution.py:1249

commit v3 on v2

--- a/solution.py
+++ b/solution.py
@@ -627,7 +627,7 @@
 
 
 def finish(
-    dkv_ref, dq_ref, tok_ref, w_ref, datt_ref, mixed_ref, done_ref, gn_ref,
+    dkv_ref, dq_ref, tok_ref, w_ref, datt_ref, datt_two, mixed_ref, done_ref, gn_ref,
     dx_ref, sqkv_ref, sout_ref, snorm_ref,
     kv_sib, kv_sum, kv_in, g_one, g_two, g_sib, g_sum, g_in,
     part, part_in, att, dkvq, nz_in, nrow, np_in, relay, sems,
@@ -652,17 +652,33 @@
         for q in (3, 2, 1, 0) for r in (3, 1, 2, 0)
     }
     att[z] = datt_ref[...]
-    att_c = Spread(go, mid, lambda j: att.at[j], z, line)
-    att_c.rest()
+    att[z ^ 2] = datt_two[...]
+    att_three = go.make(att.at[z], att.at[z], line[3])
+    go(att.at[z ^ 2], att.at[z ^ 2], line[1], only=mid, arrive=att_three.arrive)
+    go.start(att_three, only=mid)
+    att_one = go(att.at[z], att.at[z], line[1])
     nz_c = [go(gn_ref.at[pl.ds((z ^ r) * 8, 8)], nz_in.at[r - 1], line[r]) for r in (1, 2, 3)]
-    kv_out = {}
+    side, other = 1 + core, 2 - core
+    to_side = ((chip ^ side) * 2 + core, z)
+    to_other = ((chip ^ other) * 2 + core, z)
+    kv_plain, kv_pass, kv_both = {}, {}, {}
     for q in (3, 2, 1, 0):
         for r in (3, 1, 2, 0):
             kv_c[q, r].wait_recv()
             both = dkv_ref[(chip ^ r) * 2 + core, member(q), :].astype(f32) + kv_sib[q, r].astype(f32)
             kv_sum[q, r] = both.astype(bf16)
-            if r:
-                kv_out[q, r] = go(kv_sum.at[q, r], kv_in.at[q, r - 1], flat[r])
+            if r == 3:
+                kv_pass[q] = go(kv_sum.at[q, 3], kv_in.at[q, 2], to_side)
+        kv_plain[q] = go(kv_sum.at[q, side], kv_in.at[q, 0], to_side)
+
+    def add_passed(q):
+        kv_pass[q].wait_recv()
+        both = kv_sum[q, other].astype(f32) + kv_in[q, 2].astype(f32)
+        kv_sum[q, other] = both.astype(bf16)
+        kv_both[q] = go(kv_sum.at[q, other], kv_in.at[q, 1], to_other)
+
+    add_passed(3)
+    add_passed(2)
     dkvq[:, 384:640] = dq_ref[...]
 
     @pl.when(ends)
@@ -695,7 +711,6 @@
             + g_in[part_i, 1].astype(f32) + g_in[part_i, 2].astype(f32)
         )
 
-    att_c.pass_on()
     for c in nz_c:
         c.wait_recv()
     nrow[0] = gn_ref[pl.ds(z * 8, 8)] + nz_in[0] + nz_in[1] + nz_in[2]
@@ -704,10 +719,19 @@
     g_one[:, 0:128] = last[:, 0:128].astype(bf16)
     dx_c = []
     for q in (3, 2, 1, 0):
-        for r in (1, 2, 3):
-            kv_out[q, r].wait_recv()
+        if q == 1:
+            att_one.wait_recv()
+            att_three.wait_recv()
+            outs = dot_tn(att[...].reshape(512, 768), mixed_ref[...])
+            g_one[:, 128:256] = outs[:, 0:128].astype(bf16)
+            g_one[:, 256:384] = (outs[:, 128:256] + last[:, 128:256]).astype(bf16)
+            one_c = send_half(0, g_one)
+        if q >= 2:
+            add_passed(q - 2)
+        kv_plain[q].wait_recv()
+        kv_both[q].wait_recv()
         dkvq[member(q), 0:384] = (
-            kv_sum[q, 0].astype(f32) + kv_in[q, 0].astype(f32) + kv_in[q, 1].astype(f32) + kv_in[q, 2].astype(f32)
+            kv_sum[q, 0].astype(f32) + kv_in[q, 0].astype(f32) + kv_in[q, 1].astype(f32)
         ).astype(bf16)
         term = dot_nt(dkvq[member(q), :], w_ref[...])
         if q == 3:
@@ -724,16 +748,10 @@
             dx_c.append(go(part.at[1], part_in.at[1], line[2]))
         else:
             dx_ref[...] = done_ref[...] + term
+    one_out = send_sum(0, g_one, one_c)
     g_two[...] = dot_tn(tok_ref[...], dkvq[:, 0:384]).astype(bf16)
     two_c = send_half(1, g_two)
-    att_c.one.wait_recv()
-    att_c.three.wait_recv()
-    outs = dot_tn(att[...].reshape(512, 768), mixed_ref[...])
-    g_one[:, 128:256] = outs[:, 0:128].astype(bf16)
-    g_one[:, 256:384] = (outs[:, 128:256] + last[:, 128:256]).astype(bf16)
-    one_c = send_half(0, g_one)
     two_out = send_sum(1, g_two, two_c)
-    one_out = send_sum(0, g_one, one_c)
     for c in np_c:
         c.wait_recv()
     nrow[1] = nrow[0] + np_in[1] + np_in[2] + np_in[3]
@@ -757,7 +775,7 @@
     go.finish()
 
 
-def run_finish(dkv, dq, toks, w, datt, mixed, done, gn):
+def run_finish(dkv, dq, toks, w, datt, datt_two, mixed, done, gn):
     f32, bf16 = jnp.float32, jnp.bfloat16
     V = pltpu.VMEM
     return pl.pallas_call(
@@ -768,7 +786,7 @@
             jax.ShapeDtypeStruct((192, 96), f32),
             jax.ShapeDtypeStruct((1, 96), f32),
         ),
-        in_specs=[VM] * 8,
+        in_specs=[VM] * 9,
         out_specs=(VM,) * 4,
         scratch_shapes=[
             V((4, 4, 128, 384), bf16), V((4, 4, 128, 384), bf16), V((4, 3, 128, 384), bf16),
@@ -782,7 +800,7 @@
             collective_id=5, has_side_effects=True, vmem_limit_bytes=28 << 20
         ),
         name="finish",
-    )(dkv, dq, toks, w, datt, mixed, done, gn)
+    )(dkv, dq, toks, w, datt, datt_two, mixed, done, gn)
 
 
 def collect(
@@ -1248,13 +1266,14 @@
     sums = [sums[0]] + [
         lax.ppermute(sums[r], "blk", [(i, i ^ (2 * r)) for i in range(blk_n)]) for r in (1, 2, 3)
     ]
+    d_attn_two = lax.ppermute(d_attn, "head", [(i, i ^ 2) for i in range(heads_n)])
     d_q, dkv, result = run_attend_back(
         held[0], held[1], q, kv, kcode, qcode, mixed, d_heads, lse, act
     )
     input_grad, s_qkv, s_out, s_norm = run_finish(
         dkv.reshape(blk_n, group_rows, 384), d_q.reshape(group_rows, 256),
         group_tokens.reshape(group_rows, width), attn_w.reshape(width, 640),
-        d_attn, mixed.reshape(group_rows, 256), d_one, g_norm,
+        d_attn, d_attn_two, mixed.reshape(group_rows, 256), d_one, g_norm,
     )
     input_grad, s_qkv, s_out, s_norm, s_gu, s_down = run_deliver(input_grad, s_qkv, s_out, s_norm, *sums)
     return (

time: 193 us -> 189 us (0.979)
  Pallas kernels: 184 us -> 179 us
    pallas_call x1, Pallas kernels: 35.6 us -> 29.1 us  [run_finish(): pl.pallas_call(finish, out_shape=(jax.ShapeDtypeStruct((128, 768), f32),...]
  transfers between devices with their start and end apart: 6 -> 7, of which waited for: 0 -> 0; matrix products, arithmetic and copies ran while one was open for 0% -> 0% of each run, Pallas kernels for 37% -> 35%
where the time goes in v3:
time: 189 us
  Pallas kernels  179 us (95%)
  starting transfers between devices  8.56 us (5%)
    pallas_call x1, Pallas kernels, run_middle(): pl.pallas_call(middle, out_shape=(S((128, 768), bf16), S((128, 768), f32)...  75 us
    pallas_call x1, Pallas kernels, run_collect(): pl.pallas_call(collect, out_shape=(S((4, 128, 768), bf16), S((8, 96, 640)...  36.8 us
    pallas_call x1, Pallas kernels, run_finish(): pl.pallas_call(finish, out_shape=(jax.ShapeDtypeStruct((128, 768), f32),...  29.1 us
    pallas_call x1, Pallas kernels, run_attend_back(): pl.pallas_call(attend_back, out_shape=(jax.ShapeDtypeStruct((heads_n, slo...  22.1 us
    pallas_call x1, Pallas kernels, run_attend(): pl.pallas_call(attend, out_shape=(jax.ShapeDtypeStruct((heads_n, slots, 2...  14.3 us
  transfers between devices with their start and end apart: 7, of which 0 were waited for; matrix products, arithmetic and copies ran while one was open for 0% of the time, Pallas kernels for 35%

profile of v3, /device:TPU:0, one launch (start us, length us, event | category | flops | bytes accessed | tf_op | source)
XLA Modules:
  0.0 188.6 jit_solution(8129653408665059877)
XLA Ops:
  0.6 0.0 copy-start
  0.6 0.0 copy-start.2
  0.7 0.0 copy-start.3
  0.7 0.0 copy-start.1
  0.7 36.8 %collect.1 = (bf16[4,128,768]{2,1,0:T(8,128)(2,1)S(1)}, bf16[8,96,640]{2,1,0:T(8,128)(2,1)S(1)}, bf16[4,128,256]{2,1,0:T(8,128)(2,1)S(1)}, bf16[32,128,384]{2,1,...) custom-call(s32[8]{0:T(128)} %len_any.5, ...), custom_call_target="tpu_custom_call" | custom-call | tf_op jit(solution)/shard_map/collect/pallas_call | solution.py:928
  37.5 2.5 %collective-permute-start.2 = (bf16[4,96,256]{2,1,0:T(8,128)(2,1)S(1)}, bf16[4,96,256]{2,1,0:T(8,128)(2,1)S(1)}, u32[]{:S(2)}, u32[]{:S(2)}) collective-permute-start(bf16[4,96,256]{2,1,0:T(8,128)(2,1)S(1)} %get-tuple-element.45.wo_0), channel_id=1, source_target_pairs={{0,24},{4,28},{8,16},{12,20},{16,8},{20,12},{24,0},{28,4},{1,25},{... | collective-permute-start | bytes 589832 | tf_op jit(solution)/shard_map/ppermute | solution.py:1261
  40.0 1.2 collective-permute-start.1
  41.2 0.0 collective-permute-start
  41.2 14.3 %attend.1 = (bf16[4,128,256]{2,1,0:T(8,128)(2,1)S(1)}, f32[4,8,128]{2,1,0:T(8,128)S(1)}) custom-call(s32[8]{0:T(128)} %len_any.5, f32[12]{0:T(128)} %slope_any.3, bf16[4,128,256]{2,1,0:T(8,128)(2,1)S(1)} %get-tuple-element.39.q_ref, bf16[32,128,384]{2,1,0:T(8,128)(2,1)S(1)} %get-tuple-element.40.kv_ref, f32[32,128,128]{2,1,0:T(8,128)S(1)} %get-tuple-element.41.kcode_ref, ...), custom_call_target="tpu_custom_call" | custom-call | tf_op jit(solution)/shard_map/attend/pallas_call | solution.py:474
  55.5 0.0 collective-permute-done.2.wo_3
  55.5 0.0 collective-permute-done.1.wo_2
  55.5 0.0 collective-permute-done.wo_1
  55.5 0.0 copy-done
  55.5 0.0 copy-done.2
  55.5 0.0 copy-done.3
  55.6 0.0 copy-done.1
  55.6 75.0 %middle.1 = (bf16[128,768]{1,0:T(8,128)(2,1)S(1)}, f32[128,768]{1,0:T(8,128)S(1)}, bf16[128,768]{1,0:T(8,128)(2,1)S(1)}, bf16[4,128,256]{2,1,0:T(8,128)(2,1)S(1)...) custom-call(bf16[4,128,256]{2,1,0:T(8,128)(2,1)S(1)} %get-tuple-elem, ...), custom_call_target="tpu_custom_call" | custom-call | tf_op jit(solution)/shard_map/middle/pallas_call | solution.py:1180
  130.6 0.4 collective-permute-start.4
  131.0 2.0 %collective-permute-start.5 = (bf16[3,96,768]{2,1,0:T(8,128)(2,1)S(1)}, bf16[3,96,768]{2,1,0:T(8,128)(2,1)S(1)}, u32[]{:S(2)}, u32[]{:S(2)}) collective-permute-start(bf16[3,96,768]{2,1,0:T(8,128)(2,1)S(1)} %get-tuple-element.63), channel_id=1, source_target_pairs={{0,16},{4,20},{8,24},{12,28},{16,0},{20,4},{24,8},{28,12},{1,17},{... | collective-permute-start | bytes 1327112 | tf_op jit(solution)/shard_map/ppermute | solution.py:1267
  133.0 1.1 collective-permute-start.6
  134.1 1.3 collective-permute-start.3
  135.4 22.1 %attend_back.1 = (bf16[4,128,256]{2,1,0:T(8,128)(2,1)S(1)}, bf16[32,128,384]{2,1,0:T(8,128)(2,1)S(1)}, bf16[128,768]{1,0:T(8,128)(2,1)}) custom-call(s32[8]{0:T(128)} %len_any.5, f32[12]{0:T(128)} %slope_any.3, bf16[4,128,256]{2,1,0:T(8,128)(2,1)S(1)} %get-tuple-element.39.q_ref, bf16[32,128,384]{2,1,0:T(8,128)(2,1)S(1)} %get-tuple-element.40.kv_ref, ...), custom_call_target="tpu_custom_call" | custom-call | tf_op jit(solution)/shard_map/attend_back/pallas_call | solution.py:496
  157.5 0.0 collective-permute-done.3.datt_two
  157.5 29.1 %finish.1 = (f32[128,768]{1,0:T(8,128)S(1)}, f32[96,576]{1,0:T(8,128)S(1)}, f32[192,96]{1,0:T(8,128)S(1)}, f32[1,96]{1,0:T(1,128)S(1)}) custom-call(bf16[8,512,384]{2,1,0:T(8,128)(2,1)S(1)} %bitcast.10, bf16[512,256]{1,0:T(8,128)(2,1)S(1)} %bitcast.14, bf16[512,768]{1,0:T(8,128)(2,1)S(1)} %bitcast.13, bf16[768,640]{1,0:T(8,128)(2,1)S(1)} %bitcast.12, ...), custom_call_target="tpu_custom_call" | custom-call | tf_op jit(solution)/shard_map/finish/pallas_call | solution.py:781
  186.6 0.0 collective-permute-done.4.refs_5_
  186.7 0.0 collective-permute-done.5.refs_6_
  186.7 0.0 collective-permute-done.6.refs_7_
  186.7 1.8 deliver.1
Async XLA Ops:
  0.6 54.9 %copy-start = (bf16[128,768]{1,0:T(8,128)(2,1)S(1)}, bf16[128,768]{1,0:T(8,128)(2,1)}, u32[]{:S(2)}) copy-start(bf16[128,768]{1,0:T(8,128)(2,1)} %tok_any.3) | copy-start | bytes 589828
  0.6 54.9 %copy-start.2 = (bf16[128,768]{1,0:T(8,128)(2,1)S(1)}, bf16[128,768]{1,0:T(8,128)(2,1)}, u32[]{:S(2)}) copy-start(bf16[128,768]{1,0:T(8,128)(2,1)} %og_any.1) | copy-start | bytes 589828
  0.7 54.9 %copy-start.3 = (bf16[768,96]{0,1:T(8,128)(2,1)S(1)}, bf16[768,96]{0,1:T(8,128)(2,1)}, u32[]{:S(2)}) copy-start(bf16[768,96]{0,1:T(8,128)(2,1)} %param.14) | copy-start | bytes 442372
  0.7 54.9 %copy-start.1 = (bf16[2,96,768]{2,1,0:T(8,128)(2,1)S(1)}, bf16[2,96,768]{2,1,0:T(8,128)(2,1)}, u32[]{:S(2)}) copy-start(bf16[2,96,768]{2,1,0:T(8,128)(2,1)} %gu_any.1) | copy-start | bytes 884740
  37.5 18.0 %collective-permute-start.2 = (bf16[4,96,256]{2,1,0:T(8,128)(2,1)S(1)}, bf16[4,96,256]{2,1,0:T(8,128)(2,1)S(1)}, u32[]{:S(2)}, u32[]{:S(2)}) collective-permute-start(bf16[4,96,256]{2,1,0:T(8,128)(2,1)S(1)} %get-tuple-element.45.wo_0), channel_id=1, source_target_pairs={{0,24},{4,28},{8,16},{12,20},{16,8},{20,12},{24,0},{28,4},{1,25},{... | collective-permute-start | bytes 589832 | tf_op jit(solution)/shard_map/ppermute | solution.py:1261
  40.0 15.5 %collective-permute-start.1 = (bf16[4,96,256]{2,1,0:T(8,128)(2,1)S(1)}, bf16[4,96,256]{2,1,0:T(8,128)(2,1)S(1)}, u32[]{:S(2)}, u32[]{:S(2)}) collective-permute-start(bf16[4,96,256]{2,1,0:T(8,128)(2,1)S(1)} %get-tuple-element.45.wo_0), channel_id=1, source_target_pairs={{0,16},{4,20},{8,24},{12,28},{16,0},{20,4},{24,8},{28,12},{1,17},{... | collective-permute-start | bytes 589832 | tf_op jit(solution)/shard_map/ppermute | solution.py:1261
  41.2 14.4 %collective-permute-start = (bf16[4,96,256]{2,1,0:T(8,128)(2,1)S(1)}, bf16[4,96,256]{2,1,0:T(8,128)(2,1)S(1)}, u32[]{:S(2)}, u32[]{:S(2)}) collective-permute-start(bf16[4,96,256]{2,1,0:T(8,128)(2,1)S(1)} %get-tuple-element.45.wo_0), channel_id=1, source_target_pairs={{0,8},{4,12},{8,0},{12,4},{16,24},{20,28},{24,16},{28,20},{1,9},{5... | collective-permute-start | bytes 589832 | tf_op jit(solution)/shard_map/ppermute | solution.py:1261
  130.6 56.1 %collective-permute-start.4 = (bf16[3,96,768]{2,1,0:T(8,128)(2,1)S(1)}, bf16[3,96,768]{2,1,0:T(8,128)(2,1)S(1)}, u32[]{:S(2)}, u32[]{:S(2)}) collective-permute-start(bf16[3,96,768]{2,1,0:T(8,128)(2,1)S(1)} %get-tuple-element.62), channel_id=1, source_target_pairs={{0,8},{4,12},{8,0},{12,4},{16,24},{20,28},{24,16},{28,20},{1,9},{5... | collective-permute-start | bytes 1327112 | tf_op jit(solution)/shard_map/ppermute | solution.py:1267
  131.0 55.7 %collective-permute-start.5 = (bf16[3,96,768]{2,1,0:T(8,128)(2,1)S(1)}, bf16[3,96,768]{2,1,0:T(8,128)(2,1)S(1)}, u32[]{:S(2)}, u32[]{:S(2)}) collective-permute-start(bf16[3,96,768]{2,1,0:T(8,128)(2,1)S(1)} %get-tuple-element.63), channel_id=1, source_target_pairs={{0,16},{4,20},{8,24},{12,28},{16,0},{20,4},{24,8},{28,12},{1,17},{... | collective-permute-start | bytes 1327112 | tf_op jit(solution)/shard_map/ppermute | solution.py:1267
  133.0 53.7 %collective-permute-start.6 = (bf16[3,96,768]{2,1,0:T(8,128)(2,1)S(1)}, bf16[3,96,768]{2,1,0:T(8,128)(2,1)S(1)}, u32[]{:S(2)}, u32[]{:S(2)}) collective-permute-start(bf16[3,96,768]{2,1,0:T(8,128)(2,1)S(1)} %get-tuple-element.64), channel_id=1, source_target_pairs={{0,24},{4,28},{8,16},{12,20},{16,8},{20,12},{24,0},{28,4},{1,25},{... | collective-permute-start | bytes 1327112 | tf_op jit(solution)/shard_map/ppermute | solution.py:1267
  134.1 23.4 %collective-permute-start.3 = (bf16[128,768]{1,0:T(8,128)(2,1)S(1)}, bf16[128,768]{1,0:T(8,128)(2,1)S(1)}, u32[]{:S(2)}, u32[]{:S(2)}) collective-permute-start(bf16[128,768]{1,0:T(8,128)(2,1)S(1)} %get-tuple-element.54.datt_ref), channel_id=1, source_target_pairs={{0,2},{1,3},{2,0},{3,1},{4,6},{5,7},{6,4},{7,5},{8,10},{9,11},{10,... | collective-permute-start | bytes 589832 | tf_op jit(solution)/shard_map/ppermute | solution.py:1269
